TPU v7x, 128 devices: a whole 4x4x4 slice. The times are simulated.
128 devices in a mesh: atom: 32 (over y, x, core), pair: 4 (over z).
Axes of the slice: x: 4, y: 4, z: 4, core: 2. Of those that a mesh axis runs over, the one named last changes fastest.
Arguments:
- atoms: bfloat16 [1048576, 128], P(('atom', 'pair')), may hold values from -6 to 6
- pair_bias: bfloat16 [1048576, 512], P(('atom', 'pair')), may hold values from -8 to 250
- key_offsets: int32 [32768], P(('atom', 'pair')), may hold values from -64 to -32
- atom_mask: int32 [1048576], P(('atom', 'pair')), may hold values 0 or 1
- atom_token: int32 [1048576], P(('atom', 'pair')), may hold values from 0 to 131071, as said below
- norm_gain: float32 [128], replicated, may hold values from 0.25 to 1.75
- w_query: bfloat16 [128, 128], replicated, may hold values from -0.5 to 0.5
- w_key: bfloat16 [128, 128], replicated, may hold values from -0.5 to 0.5
- w_value: bfloat16 [128, 128], replicated, may hold values from -0.5 to 0.5
- w_gate: bfloat16 [128, 128], replicated, may hold values from -0.5 to 0.5
- w_out: bfloat16 [128, 128], replicated, may hold values from -0.5 to 0.5
- trans_gain: float32 [128], replicated, may hold values from 0.25 to 1.75
- w_ff_gate: bfloat16 [128, 256], replicated, may hold values from -0.5 to 0.5
- w_ff_up: bfloat16 [128, 256], replicated, may hold values from -0.5 to 0.5
- w_ff_down: bfloat16 [256, 128], replicated, may hold values from -0.375 to 0.375
- w_pool: bfloat16 [128, 384], replicated, may hold values from -0.5 to 0.5
Outputs:
- atom_out: bfloat16 [1048576, 128], P(('atom', 'pair'))
- pooled: float32 [131072, 384], P(('atom', 'pair'))
Inputs may be any that keep to these rules, and one draw needn't show every extreme that they name: `atom_token`: never falls along the atoms; every token has one or more atoms; for k > 0 the first atom of token 1024 * k lies 1 to 2048 atoms before atom 8192 * k, and a distance of 2048 occurs.
All inputs are finite; a program needn't handle non-finite values. No bound on the sum of `atom_mask` on one device may be relied on, other than what follows from the above.
Results may differ from a plain program's by a relative error of at most 0.013.
Values may be sent and summed in bfloat16 or wider, within the bound.
A program may use at most 128 MiB of HBM per device.

v0:
```python
import math

import jax
import jax.numpy as jnp
from jax import lax
from jax.sharding import PartitionSpec as P

C_ATOM = 128
HEADS = 4
QUERY_BLOCK = 32
KEY_WINDOW = 128
TOK_DEV = 1024


EPSILON = 1e-05
MASKED = -1000000000.0


def padded(cells, sides, width):
    for axis, dim in sides:
        count = lax.axis_size(axis)
        ends = count - 1
        head = lax.slice_in_dim(cells, 0, width, axis=dim)
        tail = lax.slice_in_dim(cells, cells.shape[dim] - width, cells.shape[dim], axis=dim)
        cells = jnp.concatenate(
            [
                lax.ppermute(tail, axis, [(i, (i + 1) % count) for i in range(ends)]),
                cells,
                lax.ppermute(head, axis, [((i + 1) % count, i) for i in range(ends)]),
            ],
            axis=dim,
        )
    return cells


def passed_along(value, axis, steps):
    count = lax.axis_size(axis)
    first, last = (max(0, -steps), min(count, count - steps))
    return lax.ppermute(value, axis, [(source, source + steps) for source in range(first, last)])


def layer_norm(values_in, gain_vec):
    floats = values_in.astype(jnp.float32)
    center = floats - jnp.mean(floats, axis=-1, keepdims=True)
    spread = jnp.mean(center * center, axis=-1, keepdims=True)
    return center * lax.rsqrt(spread + EPSILON) * gain_vec


def window_attention(queries, gating, pair_bias, key_offsets, kv_padded, key_live):
    query_rows, feat_width = queries.shape
    head_count = pair_bias.shape[1] // KEY_WINDOW
    head_width = feat_width // head_count
    reach = KEY_WINDOW - 2 * QUERY_BLOCK
    span_rows = 2 * reach + QUERY_BLOCK
    group_rows = math.gcd(512, query_rows)
    group_blocks = group_rows // QUERY_BLOCK
    group_count = query_rows // group_rows
    piece_count = span_rows // QUERY_BLOCK
    slot_ids = jnp.arange(KEY_WINDOW, dtype=jnp.int32)
    span_ids = jnp.arange(span_rows, dtype=jnp.int32)
    live_floats = key_live.astype(jnp.float32)

    def one_group(group_index):
        base = group_index * group_rows
        slab = lax.dynamic_slice_in_dim(kv_padded, base, group_rows + 2 * reach, 0)
        live_slab = lax.dynamic_slice_in_dim(live_floats, base, group_rows + 2 * reach, 0)
        pieces = slab.reshape(group_blocks + piece_count - 1, QUERY_BLOCK, 2 * feat_width)
        live_pieces = live_slab.reshape(group_blocks + piece_count - 1, QUERY_BLOCK)
        spans = jnp.concatenate(
            [pieces[step : step + group_blocks] for step in range(piece_count)], axis=1
        )
        live_spans = jnp.concatenate(
            [live_pieces[step : step + group_blocks] for step in range(piece_count)], axis=1
        )
        offsets = (
            lax.dynamic_slice_in_dim(key_offsets, group_index * group_blocks, group_blocks, 0)
            + reach
        )
        select = span_ids[None, None, :] == slot_ids[None, :, None] + offsets[:, None, None]
        window = jnp.einsum(
            "bjs,bsc->bjc", select.astype(jnp.bfloat16), spans, preferred_element_type=jnp.float32
        ).astype(jnp.bfloat16)
        live_keys = (
            jnp.einsum(
                "bjs,bs->bj",
                select.astype(jnp.float32),
                live_spans,
                precision=lax.Precision.HIGHEST,
            )
            > 0.5
        )
        query_part = lax.dynamic_slice_in_dim(queries, base, group_rows, 0).reshape(
            group_blocks, QUERY_BLOCK, head_count, head_width
        )
        gate_part = lax.dynamic_slice_in_dim(gating, base, group_rows, 0)
        bias_part = lax.dynamic_slice_in_dim(pair_bias, base, group_rows, 0).reshape(
            group_blocks, QUERY_BLOCK, head_count, KEY_WINDOW
        )
        key_part = window[:, :, :feat_width].reshape(
            group_blocks, KEY_WINDOW, head_count, head_width
        )
        value_part = window[:, :, feat_width:].reshape(
            group_blocks, KEY_WINDOW, head_count, head_width
        )
        scores = jnp.einsum(
            "bqhd,bkhd->bqhk", query_part, key_part, preferred_element_type=jnp.float32
        )
        scores = scores + bias_part.astype(jnp.float32)
        scores = jnp.where(live_keys[:, None, None, :], scores, MASKED)
        row_max = jnp.max(scores, axis=-1, keepdims=True)
        exp_scores = jnp.exp(scores - row_max)
        weights = (exp_scores / jnp.sum(exp_scores, axis=-1, keepdims=True)).astype(jnp.bfloat16)
        mixed = jnp.einsum(
            "bqhk,bkhd->bqhd", weights, value_part, preferred_element_type=jnp.float32
        )
        return (mixed.reshape(group_rows, feat_width) * gate_part).astype(jnp.bfloat16)

    outputs = lax.map(one_group, jnp.arange(group_count, dtype=jnp.int32))
    return outputs.reshape(query_rows, feat_width)


def pool_tiles(projected, token_ids, keep_mask, token_base, token_span):
    atom_rows, feat_width = projected.shape
    tile_rows = math.gcd(512, atom_rows)
    tile_count = atom_rows // tile_rows
    slot_ids = jnp.arange(tile_rows, dtype=jnp.int32)
    proj_tiles = projected.reshape(tile_count, tile_rows, feat_width)
    id_tiles = token_ids.reshape(tile_count, tile_rows)
    keep_tiles = keep_mask.reshape(tile_count, tile_rows)

    def add_tile(tile_index, carry):
        token_sums, token_counts = carry
        proj_tile = proj_tiles[tile_index]
        ids_tile = id_tiles[tile_index]
        keep_tile = keep_tiles[tile_index]
        first_token = jnp.clip(ids_tile[0], token_base, token_base + token_span)
        owned = keep_tile & (ids_tile >= token_base) & (ids_tile < token_base + token_span)
        table = ((ids_tile[None, :] - first_token == slot_ids[:, None]) & owned[None, :]).astype(
            jnp.bfloat16
        )
        tile_sums = jnp.dot(table, proj_tile, preferred_element_type=jnp.float32)
        tile_counts = jnp.sum(table.astype(jnp.float32), axis=1)
        offset = first_token - token_base
        token_sums = lax.dynamic_update_slice_in_dim(
            token_sums,
            lax.dynamic_slice_in_dim(token_sums, offset, tile_rows, 0) + tile_sums,
            offset,
            0,
        )
        token_counts = lax.dynamic_update_slice_in_dim(
            token_counts,
            lax.dynamic_slice_in_dim(token_counts, offset, tile_rows, 0) + tile_counts,
            offset,
            0,
        )
        return (token_sums, token_counts)

    initial = (
        jnp.zeros((token_span + tile_rows, feat_width), jnp.float32),
        jnp.zeros((token_span + tile_rows,), jnp.float32),
    )
    token_sums, token_counts = lax.fori_loop(0, tile_count, add_tile, initial)
    return (token_sums[:token_span], token_counts[:token_span])


def shards(
    atoms,
    pair_bias,
    key_offsets,
    atom_mask,
    atom_token,
    norm_gain,
    w_query,
    w_key,
    w_value,
    w_gate,
    w_out,
    trans_gain,
    w_ff_gate,
    w_ff_up,
    w_ff_down,
    w_pool,
):
    reach = KEY_WINDOW - 2 * QUERY_BLOCK
    device = lax.axis_index(("atom", "pair"))
    normed = layer_norm(atoms, norm_gain).astype(jnp.bfloat16)
    query_scale = 1.0 / math.sqrt(C_ATOM // HEADS)
    queries = (jnp.dot(normed, w_query, preferred_element_type=jnp.float32) * query_scale).astype(
        jnp.bfloat16
    )
    gating = jax.nn.sigmoid(jnp.dot(normed, w_gate, preferred_element_type=jnp.float32))
    w_keyvalue = jnp.concatenate([w_key, w_value], axis=1)
    key_live = padded(atom_mask, ((("atom", "pair"), 0),), reach) == 1
    keys_values = jnp.dot(normed, w_keyvalue, preferred_element_type=jnp.float32).astype(
        jnp.bfloat16
    )
    kv_padded = padded(keys_values, ((("atom", "pair"), 0),), reach)
    attended = window_attention(queries, gating, pair_bias, key_offsets, kv_padded, key_live)
    updated = (
        atoms.astype(jnp.float32) + jnp.dot(attended, w_out, preferred_element_type=jnp.float32)
    ).astype(jnp.bfloat16)
    second = layer_norm(updated, trans_gain).astype(jnp.bfloat16)
    hidden = (
        jax.nn.silu(jnp.dot(second, w_ff_gate, preferred_element_type=jnp.float32))
        * jnp.dot(second, w_ff_up, preferred_element_type=jnp.float32)
    ).astype(jnp.bfloat16)
    atom_out = (
        updated.astype(jnp.float32) + jnp.dot(hidden, w_ff_down, preferred_element_type=jnp.float32)
    ).astype(jnp.bfloat16)
    own_keep = atom_mask == 1
    projected = jax.nn.relu(jnp.dot(atom_out, w_pool, preferred_element_type=jnp.float32)).astype(
        jnp.bfloat16
    )
    block_sums, block_counts = pool_tiles(
        projected, atom_token, own_keep, device * TOK_DEV, 2 * TOK_DEV
    )
    from_below = (
        passed_along(block_sums[TOK_DEV:].astype(jnp.bfloat16), ("atom", "pair"), 1).astype(
            jnp.float32
        ),
        passed_along(block_counts[TOK_DEV:].astype(jnp.bfloat16), ("atom", "pair"), 1).astype(
            jnp.float32
        ),
    )
    token_sums = block_sums[:TOK_DEV] + from_below[0]
    token_counts = block_counts[:TOK_DEV] + from_below[1]
    pooled = token_sums / jnp.maximum(token_counts, 1.0)[:, None]
    return (atom_out, pooled)


def solution(mesh):
    in_specs = (
        P(("atom", "pair"), None),
        P(("atom", "pair"), None),
        P(("atom", "pair")),
        P(("atom", "pair")),
        P(("atom", "pair")),
        P(),
        P(),
        P(),
        P(),
        P(),
        P(),
        P(),
        P(),
        P(),
        P(),
        P(),
    )
    out_specs = (P(("atom", "pair"), None), P(("atom", "pair"), None))
    return jax.shard_map(shards, mesh=mesh, in_specs=in_specs, out_specs=out_specs, check_vma=False)
```

profile of v0, /device:TPU:9, one launch (start us, length us, event | category | flops | bytes accessed | tf_op | source)
XLA Modules:
  0.0 493.5 jit_solution(10999407286604863396)
XLA Ops:
  11.6 4.6 collective-permute-start.1
  18.2 4.9 collective-permute-start.3
  29.3 9.5 %pad_maximum_fusion = bf16[8320,256]{1,0:T(8,128)(2,1)} fusion(bf16[64,256]{1,0:T(8,128)(2,1)S(1)} %collective-permute-done.1, bf16[8192,256]{1,0:T(8,128)(2,1)} %copy-done.3, bf16[64,256]{1,0:T(8,128)(2,1)S(1)} %collective-permute-done), kind=kLoop, calls=%fused_computation.73 | loop fusion | flops 12779520 | bytes 8519680 | tf_op jit(solution)/shard_map/concatenate | solution.py:25
  38.8 301.2 %while.28 = (s32[]{:T(128)}, bf16[16,512,128]{2,1,0:T(8,128)(2,1)}, s32[16]{0:T(128)S(1)}, s32[256]{0:T(256)S(1)}, bf16[8320,256]{1,0:T(8,128)(2,1)}, /*index=5*...) while((s32[]{:T(128)}, bf16[16,512,128]{2,1,0:T(8,128)(2,1)}, ...), condition=%wide.region_5.6_spmd.clone, body=%wide.region_2.5_spmd.clone.sunk | while | flops 208673056 | bytes 25043020 | solution.py:118
  51.0 3.6 convolution_bitcast_fusion.3
  69.9 3.6 convolution_bitcast_fusion.3
  88.8 3.6 convolution_bitcast_fusion.3
  107.6 3.6 convolution_bitcast_fusion.3
  126.4 3.6 convolution_bitcast_fusion.3
  145.2 3.6 convolution_bitcast_fusion.3
  163.9 3.6 convolution_bitcast_fusion.3
  182.7 3.6 convolution_bitcast_fusion.3
  201.4 3.6 convolution_bitcast_fusion.3
  220.3 3.6 convolution_bitcast_fusion.3
  239.1 3.6 convolution_bitcast_fusion.3
  258.0 3.6 convolution_bitcast_fusion.3
  276.9 3.6 convolution_bitcast_fusion.3
  295.7 3.6 convolution_bitcast_fusion.3
  314.4 3.6 convolution_bitcast_fusion.3
  345.0 4.6 fusion.46
  349.6 8.7 %fusion.34 = bf16[8192,128]{0,1:T(8,128)(2,1)S(1)} fusion(f32[8192,128]{0,1:T(8,128)} %copy-done.1, bf16[256,128]{1,0:T(8,128)(2,1)S(1)} %copy-done.9, bf16[128,256]{1,0:T(8,128)(2,1)S(1)} %copy-done.10, f32[8192,256]{1,0:T(8,128)} %fusion.46, f32[128]{0:T(128)S(1)} %copy-done.8, f32[8192]{0:T(1024)S(1)} %add_rsqrt_fusion, f32[8192]{0:T(1024)S(1)} %broadcast_multiply_fusion), kind=kOutput, calls=%fused_computation.67 | convolution fusion | flops 1092616192 | bytes 14877184 | tf_op jit(solution)/shard_map/dot_general | solution.py:208
  358.3 4.5 maximum_convert_fusion
  365.0 100.9 %while.29 = (s32[]{:T(128)}, f32[2560,384]{1,0:T(8,128)}, f32[2560]{0:T(1024)S(1)}, s32[16,512]{1,0:T(8,128)S(1)}, s32[]{:T(128)}, /*index=5*/s32[]{:T(128)}, pr...) while((s32[]{:T(128)}, f32[2560,384]{1,0:T(8,128)}, ...), condition=%wide.region_10.11_spmd.clone, body=%wide.region_8.10_spmd.clone.sunk | while | flops 203360768 | bytes 3560159 | solution.py:162
  473.7 16.8 %collective-permute-done.5 = bf16[1024]{0:T(1024)(128)(2,1)S(1)} collective-permute-done((bf16[1024]{0:T(1024)(128)(2,1)S(1)}, bf16[1024]{0:T(1024)(128)(2,1)S(1)}, u32[]{:S(2)}, u32[]{:S(2)}) %collective-permute-start.5) | collective-permute-done | bytes 2080 | tf_op jit(solution)/shard_map/ppermute | solution.py:39
  (760 shorter events, 350.4 us)
Async XLA Ops:
  0.6 357.7 %copy-start = (bf16[128,384]{1,0:T(8,128)(2,1)S(1)}, bf16[128,384]{1,0:T(8,128)(2,1)}, u32[]{:S(2)}) copy-start(bf16[128,384]{1,0:T(8,128)(2,1)} %param.35) | copy-start | bytes 294916
  0.6 4.0 copy-start.16
  0.7 4.0 copy-start.12
  0.7 4.0 copy-start.11
  3.6 23.0 %copy-start.2 = (bf16[8192,128]{0,1:T(8,128)(2,1)}, bf16[8192,128]{0,1:T(8,128)(2,1)S(1)}, u32[]{:S(2)}) copy-start(bf16[8192,128]{0,1:T(8,128)(2,1)S(1)} %copy.49) | copy-start | bytes 6291460
  4.7 11.6 %copy-start.4 = (s32[8192]{0:T(1024)S(1)}, s32[8192]{0:T(1024)}, u32[]{:S(2)}) copy-start(s32[8192]{0:T(1024)} %param.23) | copy-start | bytes 98308
  4.7 18.5 %copy-start.13 = (bf16[128,128]{1,0:T(8,128)(2,1)S(1)}, bf16[128,128]{1,0:T(8,128)(2,1)}, u32[]{:S(2)}) copy-start(bf16[128,128]{1,0:T(8,128)(2,1)} %param.29) | copy-start | bytes 98308
  6.1 2.0 copy-start.3
  8.1 21.2 %collective-permute-start = (bf16[64,256]{1,0:T(8,128)(2,1)S(1)}, bf16[64,256]{1,0:T(8,128)(2,1)S(1)}, u32[]{:S(2)}, u32[]{:S(2)}) collective-permute-start(bf16[64,256]{1,0:T(8,128)(2,1)S(1)} %get-tuple-element.359), channel_id=1, source_target_pairs={{0,1},{1,2},{2,3},{3,4},{4,5},{5,6},{6,7},{7,8},{8,9},{9,10},{10,1... | collective-permute-start | bytes 98312 | tf_op jit(solution)/shard_map/ppermute | solution.py:27
  11.6 17.7 %collective-permute-start.1 = (bf16[64,256]{1,0:T(8,128)(2,1)S(1)}, bf16[64,256]{1,0:T(8,128)(2,1)S(1)}, u32[]{:S(2)}, u32[]{:S(2)}) collective-permute-start(bf16[64,256]{1,0:T(8,128)(2,1)S(1)} %get-tuple-element.360), channel_id=1, source_target_pairs={{1,0},{2,1},{3,2},{4,3},{5,4},{6,5},{7,6},{8,7},{9,8},{10,9},{11,1... | collective-permute-start | bytes 98312 | tf_op jit(solution)/shard_map/ppermute | solution.py:29
  16.3 12.8 %collective-permute-start.2 = (s32[64]{0:T(128)S(1)}, s32[64]{0:T(128)S(1)}, u32[]{:S(2)}, u32[]{:S(2)}) collective-permute-start(s32[64]{0:T(128)S(1)} %get-tuple-element.362), channel_id=1, source_target_pairs={{0,1},{1,2},{2,3},{3,4},{4,5},{5,6},{6,7},{7,8},{8,9},{9,10},{10,1... | collective-permute-start | bytes 776 | tf_op jit(solution)/shard_map/ppermute | solution.py:27
  18.2 10.9 %collective-permute-start.3 = (s32[64]{0:T(128)S(1)}, s32[64]{0:T(128)S(1)}, u32[]{:S(2)}, u32[]{:S(2)}) collective-permute-start(s32[64]{0:T(128)S(1)} %get-tuple-element.361), channel_id=1, source_target_pairs={{1,0},{2,1},{3,2},{4,3},{5,4},{6,5},{7,6},{8,7},{9,8},{10,9},{11,1... | collective-permute-start | bytes 776 | tf_op jit(solution)/shard_map/ppermute | solution.py:29
  23.1 3.5 copy-start.14
  26.6 2.5 copy-start.7
  29.3 9.5 %copy-start.15 = (s32[256]{0:T(256)S(1)}, s32[256]{0:T(256)}, u32[]{:S(2)}) copy-start(s32[256]{0:T(256)} %param.22) | copy-start | bytes 3076
  38.8 301.2 %copy-start.6 = (bf16[128,128]{1,0:T(8,128)(2,1)S(1)}, bf16[128,128]{1,0:T(8,128)(2,1)}, u32[]{:S(2)}) copy-start(bf16[128,128]{1,0:T(8,128)(2,1)} %param.30) | copy-start | bytes 98308
  343.0 1.9 copy-start.1
  343.0 1.9 copy-start.5
  343.0 1.9 copy-start.8
  345.0 4.7 copy-start.9
  345.0 4.7 copy-start.10
  467.4 23.1 %collective-permute-start.4 = (bf16[1024,384]{1,0:T(8,128)(2,1)S(1)}, bf16[1024,384]{1,0:T(8,128)(2,1)}, u32[]{:S(2)}, u32[]{:S(2)}) collective-permute-start(bf16[1024,384]{1,0:T(8,128)(2,1)S(1)} %slice.188), channel_id=1, source_target_pairs={{0,1},{1,2},{2,3},{3,4},{4,5},{5,6},{6,7},{7,8},{8,9},{9,10},{10,1... | collective-permute-start | bytes 2359304 | tf_op jit(solution)/shard_map/ppermute | solution.py:39
  469.4 21.1 %collective-permute-start.5 = (bf16[1024]{0:T(1024)(128)(2,1)S(1)}, bf16[1024]{0:T(1024)(128)(2,1)S(1)}, u32[]{:S(2)}, u32[]{:S(2)}) collective-permute-start(bf16[1024]{0:T(1024)(128)(2,1)S(1)} %slice.189), channel_id=1, source_target_pairs={{0,1},{1,2},{2,3},{3,4},{4,5},{5,6},{6,7},{7,8},{8,9},{9,10},{10,1... | collective-permute-start | bytes 6152 | tf_op jit(solution)/shard_map/ppermute | solution.py:39
where the time goes:
time: 498 us; the launch traced here: 494 us
  local copies, waits for them, and re-layouts  210 us (42%)
  matrix products  159 us (32%)
  other arithmetic  54.1 us (11%)
  loops' own time  34.1 us (7%)
  starting transfers between devices  18.7 us (4%)
  waiting for transfers between devices  16.8 us (3%)
    dot_general x16, matrix products, one_group(): jnp.einsum('bqhk,bkhd->bqhd', weights, value_part, preferred_element_type...  58.1 us
    dynamic_update_slice x16, local copies, waits for them, and re-layouts, add_tile(): lax.dynamic_update_slice_in_dim(token_sums, lax.dynamic_slice_in_dim(toke...  46.3 us
    dot_general x16, matrix products, add_tile(): tile_sums = jnp.dot(table, proj_tile, preferred_element_type=jnp.float32)  27.5 us
    slice x16, local copies, waits for them, and re-layouts, one_group(): pieces[step:step + group_blocks]  25.4 us
    another operation x1, loops' own time, window_attention(): outputs = lax.map(one_group, jnp.arange(group_count, dtype=jnp.int32))  23.2 us
    dot_general x16, matrix products, one_group(): jnp.einsum('bqhd,bkhd->bqhk', query_part, key_part, preferred_element_typ...  21.3 us
    slice x32, local copies, waits for them, and re-layouts, one_group(): window[:, :, :feat_width]  20.7 us
    convert_element_type x16, other arithmetic, one_group(): scores = scores + bias_part.astype(jnp.float32)  18.7 us
  transfers between devices with their start and end apart: 6, of which 1 were waited for; matrix products, arithmetic and copies ran while one was open for 2% of the time, Pallas kernels for 0%

commit v1 on v0

v1 whole, which is shorter than its diff:
```python
import functools
import math

import jax
import jax.numpy as jnp
from jax import lax
from jax.experimental import pallas as pl
from jax.experimental.pallas import tpu as pltpu
from jax.sharding import PartitionSpec as P

C_ATOM = 128
HEADS = 4
HEAD = C_ATOM // HEADS
HIDDEN = 256
C_TOKEN = 384
QUERY_BLOCK = 32
KEY_WINDOW = 128
ATOM_DEV = 8192
REACH = 64
TOK_DEV = 1024
EPSILON = 1e-05
MASKED = -1000000000.0
LIVE = 3e38

TILE = 512
BLOCKS = TILE // QUERY_BLOCK
SPAN = TILE + 2 * REACH
TILES = ATOM_DEV // TILE
WIN = 128
OWN_ROWS = TOK_DEV + WIN
ALL_ROWS = 2 * TOK_DEV + WIN
SUM_COLS = C_TOKEN + 128
PEN_OFF = 8
PEN_ROWS = ATOM_DEV // 128 + 2 * PEN_OFF
QSCALE = 1.0 / math.sqrt(HEAD)

NT = (((1,), (1,)), ((), ()))
AXES = ("atom", "pair")


def dot(a, b):
    return jnp.dot(a, b, preferred_element_type=jnp.float32)


def layer_norm(floats, gain):
    center = floats - jnp.mean(floats, axis=-1, keepdims=True)
    spread = jnp.mean(center * center, axis=-1, keepdims=True)
    return center * lax.rsqrt(spread + EPSILON) * gain


def sigmoid(x):
    return 0.5 * jnp.tanh(0.5 * x) + 0.5


def block_kernel(kind, tile_of, count, *refs):
    it = iter(refs)
    koff, tok = next(it), next(it)
    cur, prev, nxt, bias, mask, ids = (next(it) for _ in range(6))
    g1, wq, wk, wv, wg, wo, g2, wfg, wfu, wfd, wp = (next(it) for _ in range(11))
    below = above = acc_in = arrived = None
    if kind["halo"]:
        below, above = next(it), next(it)
    if kind["acc_in"]:
        acc_in = next(it)
    if kind["final"]:
        arrived = next(it)
    if kind["chain"]:
        next(it)
    out = next(it)
    acc_out = up_out = pooled = None
    if kind["final"]:
        pooled = next(it)
    else:
        acc_out = next(it)
    if kind["tail"]:
        up_out = next(it)
    k_s, v_s, pen_s, q_s, gate_s, att_s, proj_s, acc_s = (next(it) for _ in range(8))

    step = pl.program_id(0)
    tile = tile_of(step)
    base = (lax.axis_index("atom") * lax.axis_size("pair") + lax.axis_index("pair")) * TOK_DEV

    @pl.when(step == 0)
    def _():
        own = mask[...]
        pen_s[PEN_OFF : PEN_OFF + ATOM_DEV // 128, :] = jnp.where(own == 1, LIVE, MASKED)
        edge = jnp.full((PEN_OFF, 128), MASKED, jnp.float32)
        pen_s[0:PEN_OFF, :] = edge
        pen_s[PEN_ROWS - PEN_OFF :, :] = edge
        if kind["halo"]:
            low = below[REACH : REACH + 1, :].astype(jnp.float32)
            high = above[REACH : REACH + 1, :].astype(jnp.float32)
            pen_s[PEN_OFF - 1 : PEN_OFF, :] = jnp.where(low > 0.5, LIVE, MASKED)
            pen_s[PEN_ROWS - PEN_OFF : PEN_ROWS - PEN_OFF + 1, :] = jnp.where(
                high > 0.5, LIVE, MASKED
            )
        proj_s[:, C_TOKEN:] = jnp.ones((TILE, 128), jnp.bfloat16)
        if kind["acc_in"]:
            acc_s[0:OWN_ROWS, :] = acc_in[...]
            if kind["tail"]:
                acc_s[OWN_ROWS:, :] = jnp.zeros((ALL_ROWS - OWN_ROWS, SUM_COLS), jnp.float32)
        else:
            acc_s[...] = jnp.zeros(acc_s.shape, jnp.float32)

    first, last = prev[...], nxt[...]
    if kind["halo"]:
        first = jnp.where(tile == 0, below[0:REACH, :], first)
        last = jnp.where(tile == TILES - 1, above[0:REACH, :], last)
    rows = jnp.concatenate([first, cur[...], last], axis=0)
    normed = layer_norm(rows.astype(jnp.float32), g1[...]).astype(jnp.bfloat16)
    kv = dot(normed, jnp.concatenate([wk[...], wv[...]], axis=1))
    k_s[...] = kv[:, :C_ATOM]
    v_s[...] = kv[:, C_ATOM:]
    mid = normed[REACH : REACH + TILE]
    qg = dot(mid, jnp.concatenate([wq[...], wg[...]], axis=1))
    q_s[...] = (qg[:, :C_ATOM] * QSCALE).astype(jnp.bfloat16)
    gate_s[...] = sigmoid(qg[:, C_ATOM:])

    lane = lax.broadcasted_iota(jnp.int32, (1, C_ATOM), 1)
    heads = [(lane // HEAD == h) for h in range(HEADS)]
    head_ones = [m.astype(jnp.bfloat16) for m in heads]
    eye = (
        lax.broadcasted_iota(jnp.int32, (KEY_WINDOW, KEY_WINDOW), 0)
        == lax.broadcasted_iota(jnp.int32, (KEY_WINDOW, KEY_WINDOW), 1)
    ).astype(jnp.bfloat16)
    ones = jnp.ones((KEY_WINDOW, 128), jnp.bfloat16)
    for blk in range(BLOCKS):
        off = koff[tile * BLOCKS + blk]
        r0 = blk * QUERY_BLOCK
        window = pl.ds(r0 + REACH + off, KEY_WINDOW)
        keys = k_s[window, :].astype(jnp.bfloat16)
        values = v_s[window, :].astype(jnp.bfloat16)
        q = q_s[r0 : r0 + QUERY_BLOCK, :]
        stacked = jnp.concatenate([q * m for m in head_ones], axis=0)
        biases = jnp.concatenate(
            [
                bias[r0 : r0 + QUERY_BLOCK, h * KEY_WINDOW : (h + 1) * KEY_WINDOW]
                for h in range(HEADS)
            ],
            axis=0,
        )
        scores = lax.dot_general(
            jnp.concatenate([stacked, biases], axis=1),
            jnp.concatenate([keys, eye], axis=1),
            NT,
            preferred_element_type=jnp.float32,
        )
        place = tile * TILE + (r0 + PEN_OFF * 128) + off
        turn = 128 - (place & 127)
        pair = pen_s[pl.ds(place >> 7, 2), :]
        turned = pltpu.roll(pair, turn & 127, 1)
        limit = jnp.where(lane < turn, turned[0:1], turned[1:2])
        scores = jnp.minimum(scores, limit)
        top = jnp.max(scores, axis=1, keepdims=True)
        weights = jnp.exp(scores - top).astype(jnp.bfloat16)
        mixed = dot(weights, jnp.concatenate([values, ones], axis=1))
        num = mixed[0:QUERY_BLOCK, :C_ATOM]
        den = mixed[0:QUERY_BLOCK, C_ATOM:]
        for h in range(1, HEADS):
            part = mixed[h * QUERY_BLOCK : (h + 1) * QUERY_BLOCK]
            num = jnp.where(heads[h], part[:, :C_ATOM], num)
            den = jnp.where(heads[h], part[:, C_ATOM:], den)
        att_s[r0 : r0 + QUERY_BLOCK, :] = (
            num / den * gate_s[r0 : r0 + QUERY_BLOCK, :]
        ).astype(jnp.bfloat16)

    updated = (cur[...].astype(jnp.float32) + dot(att_s[...], wo[...])).astype(jnp.bfloat16)
    wide = updated.astype(jnp.float32)
    second = layer_norm(wide, g2[...]).astype(jnp.bfloat16)
    gated = dot(second, wfg[...])
    hidden = (gated * sigmoid(gated) * dot(second, wfu[...])).astype(jnp.bfloat16)
    atom_out = (wide + dot(hidden, wfd[...])).astype(jnp.bfloat16)
    out[...] = atom_out
    proj_s[:, :C_TOKEN] = jnp.maximum(dot(atom_out, wp[...]), 0.0).astype(jnp.bfloat16)

    row0 = tile * (TILE // 128)
    local = ids[pl.ds(row0, TILE // 128), :] - base
    local = jnp.where(mask[pl.ds(row0, TILE // 128), :] == 1, local, -1)
    row = jnp.concatenate([local[i : i + 1] for i in range(TILE // 128)], axis=1)
    head_tok = tok[tile * TILE] - base
    tail_tok = tok[tile * TILE + TILE - 1] - base
    start = (head_tok // 8) * 8
    slots = lax.broadcasted_iota(jnp.int32, (WIN, TILE), 0)

    def add(i, carry):
        at = pl.multiple_of(start + i * WIN, 8)
        table = (row - at == slots).astype(jnp.bfloat16)
        acc_s[pl.ds(at, WIN), :] += dot(table, proj_s[...])
        return carry

    lax.fori_loop(0, (tail_tok - start) // WIN + 1, add, 0)

    @pl.when(step == count - 1)
    def _():
        if kind["final"]:
            got = arrived[...].astype(jnp.float32)
            counts = got[:, C_TOKEN:]
            counts = counts + pltpu.roll(counts, 64, 1) + acc_s[0:TOK_DEV, C_TOKEN:]
            sums = got[:, :C_TOKEN] + acc_s[0:TOK_DEV, :C_TOKEN]
            counts = jnp.maximum(counts, 1.0)
            pooled[...] = sums / jnp.concatenate([counts] * (C_TOKEN // 128), axis=1)
        else:
            acc_out[...] = acc_s[0:OWN_ROWS, :]
        if kind["tail"]:
            up_out[:, :C_TOKEN] = acc_s[TOK_DEV : 2 * TOK_DEV, :C_TOKEN].astype(jnp.bfloat16)
            counts = acc_s[TOK_DEV : 2 * TOK_DEV, C_TOKEN:]
            high = counts.astype(jnp.bfloat16).astype(jnp.float32)
            up_out[:, C_TOKEN:] = jnp.where(lane < 64, high, counts - high).astype(jnp.bfloat16)


def run_tiles(ranges, kind, args, extra, chained):
    koff, tok, atoms, pair_bias, mask2, ids2, weights = args
    count = sum(b - a for a, b in ranges)

    def tile_of(step):
        done, tile = 0, 0
        for i, (a, b) in enumerate(ranges):
            tile = step + (a - done) if i == 0 else jnp.where(step >= done, step + (a - done), tile)
            done += b - a
        return tile

    per = TILE // REACH
    blocks = ATOM_DEV // REACH
    whole = lambda shape: pl.BlockSpec(shape, lambda t, *_: (0,) * len(shape))
    in_specs = [
        pl.BlockSpec((TILE, C_ATOM), lambda t, *_: (tile_of(t), 0)),
        pl.BlockSpec((REACH, C_ATOM), lambda t, *_: (jnp.maximum(tile_of(t) * per - 1, 0), 0)),
        pl.BlockSpec(
            (REACH, C_ATOM), lambda t, *_: (jnp.minimum(tile_of(t) * per + per, blocks - 1), 0)
        ),
        pl.BlockSpec((TILE, HEADS * KEY_WINDOW), lambda t, *_: (tile_of(t), 0)),
        whole(mask2.shape),
        whole(ids2.shape),
    ] + [whole(w.shape) for w in weights]
    operands = [koff, tok, atoms, atoms, atoms, pair_bias, mask2, ids2, *weights, *extra]
    in_specs += [whole(e.shape) for e in extra]
    aliases = {}
    if kind["chain"]:
        in_specs.append(pl.BlockSpec(memory_space=pl.ANY))
        aliases = {len(operands): 0}
        operands.append(chained)
    out_shape = [jax.ShapeDtypeStruct((ATOM_DEV, C_ATOM), jnp.bfloat16)]
    out_specs = [pl.BlockSpec((TILE, C_ATOM), lambda t, *_: (tile_of(t), 0))]
    if kind["final"]:
        out_shape.append(jax.ShapeDtypeStruct((TOK_DEV, C_TOKEN), jnp.float32))
    else:
        out_shape.append(jax.ShapeDtypeStruct((OWN_ROWS, SUM_COLS), jnp.float32))
    if kind["tail"]:
        out_shape.append(jax.ShapeDtypeStruct((TOK_DEV, SUM_COLS), jnp.bfloat16))
    out_specs += [whole(o.shape) for o in out_shape[1:]]
    return pl.pallas_call(
        functools.partial(block_kernel, kind, tile_of, count),
        grid_spec=pltpu.PrefetchScalarGridSpec(
            num_scalar_prefetch=2,
            grid=(count,),
            in_specs=in_specs,
            out_specs=out_specs,
            scratch_shapes=[
                pltpu.VMEM((SPAN, C_ATOM), jnp.float32),
                pltpu.VMEM((SPAN, C_ATOM), jnp.float32),
                pltpu.VMEM((PEN_ROWS, 128), jnp.float32),
                pltpu.VMEM((TILE, C_ATOM), jnp.bfloat16),
                pltpu.VMEM((TILE, C_ATOM), jnp.float32),
                pltpu.VMEM((TILE, C_ATOM), jnp.bfloat16),
                pltpu.VMEM((TILE, SUM_COLS), jnp.bfloat16),
                pltpu.VMEM((ALL_ROWS if kind["tail"] else OWN_ROWS, SUM_COLS), jnp.float32),
            ],
        ),
        out_shape=out_shape,
        input_output_aliases=aliases,
        compiler_params=pltpu.CompilerParams(
            dimension_semantics=("arbitrary",), vmem_limit_bytes=48 * 1024 * 1024
        ),
        cost_estimate=pl.CostEstimate(
            flops=count * TILE * 2000000, bytes_accessed=count * TILE * 1600, transcendentals=0
        ),
    )(*operands)


def moved(value, steps):
    count = lax.axis_size(AXES)
    first, last = max(0, -steps), min(count, count - steps)
    return lax.ppermute(value, AXES, [(i, i + steps) for i in range(first, last)])


def shards(
    atoms,
    pair_bias,
    key_offsets,
    atom_mask,
    atom_token,
    norm_gain,
    w_query,
    w_key,
    w_value,
    w_gate,
    w_out,
    trans_gain,
    w_ff_gate,
    w_ff_up,
    w_ff_down,
    w_pool,
):
    mask2 = atom_mask.reshape(ATOM_DEV // 128, 128)
    ids2 = atom_token.reshape(ATOM_DEV // 128, 128)
    marks = atom_mask.astype(jnp.bfloat16)

    def edge(rows, live):
        return jnp.concatenate([rows, jnp.broadcast_to(live[None], (16, 128))], axis=0)

    below = moved(edge(atoms[-REACH:], marks[-128:]), 1)
    above = moved(edge(atoms[:REACH], marks[:128]), -1)
    weights = (
        norm_gain[None],
        w_query,
        w_key,
        w_value,
        w_gate,
        w_out,
        trans_gain[None],
        w_ff_gate,
        w_ff_up,
        w_ff_down,
        w_pool,
    )
    args = (key_offsets, atom_token, atoms, pair_bias, mask2, ids2, weights)
    flags = dict(halo=False, acc_in=False, final=False, chain=False, tail=False)
    quarter = TILES // 4
    out, acc = run_tiles([(quarter, 2 * quarter)], flags, args, [], None)
    out, acc, up = run_tiles(
        [(3 * quarter, TILES)],
        {**flags, "halo": True, "acc_in": True, "chain": True, "tail": True},
        args,
        [below, above, acc],
        out,
    )
    arrived = moved(up, 1)
    out, acc = run_tiles(
        [(2 * quarter, 3 * quarter)],
        {**flags, "acc_in": True, "chain": True},
        args,
        [acc],
        out,
    )
    out, pooled = run_tiles(
        [(0, quarter)],
        {**flags, "halo": True, "acc_in": True, "chain": True, "final": True},
        args,
        [below, above, acc, arrived],
        out,
    )
    return (out, pooled)


def solution(mesh):
    rows = P(("atom", "pair"))
    wide = P(("atom", "pair"), None)
    in_specs = (wide, wide, rows, rows, rows) + (P(),) * 11
    return jax.shard_map(
        shards, mesh=mesh, in_specs=in_specs, out_specs=(wide, wide), check_vma=False
    )
```

time: 498 us -> 99.9 us (0.20)
  local copies, waits for them, and re-layouts: 210 us -> 15.9 us
  matrix products: 159 us -> 0 us
  Pallas kernels: 0 us -> 59.9 us
  other arithmetic: 54.1 us -> 0.77 us
  loops' own time: 34.1 us -> 0 us
  starting transfers between devices: 18.7 us -> 10.1 us
  waiting for transfers between devices: 16.8 us -> 11.5 us
    dot_general x87 -> x0, matrix products: 159 us -> none  [the longest x16 58.1 us: one_group(): jnp.einsum('bqhk,bkhd->bqhd', weights, value_part, preferred_element_type...]
    slice x180 -> x2, local copies, waits for them, and re-layouts: 67.7 us -> 0.75 us  [shards(): above = moved(edge(atoms[:REACH], marks[:128]), -1)]
    pallas_call x0 -> x4, Pallas kernels: none -> 59.9 us  [run_tiles(): pl.pallas_call(functools.partial(block_kernel, kind, tile_of, count), gri...]
    dynamic_update_slice x48 -> x0, local copies, waits for them, and re-layouts: 59 us -> none  [the longest x16 46.3 us: add_tile(): lax.dynamic_update_slice_in_dim(token_sums, lax.dynamic_slice_in_dim(toke...]
    dynamic_slice x80 -> x0, local copies, waits for them, and re-layouts: 42.8 us -> none  [the longest x32 17.5 us: one_group(): gate_part = lax.dynamic_slice_in_dim(gating, base, group_rows, 0)]
    another operation x2 -> x0, loops' own time: 34.1 us -> none  [the longest x1 23.2 us: window_attention(): outputs = lax.map(one_group, jnp.arange(group_count, dtype=jnp.int32))]
    convert_element_type x17 -> x1, other arithmetic: 18.7 us -> 0.76 us  [shards(): marks = atom_mask.astype(jnp.bfloat16)]
    reshape x34 -> x0, local copies, waits for them, and re-layouts: 10.6 us -> none  [the longest x16 6.78 us: one_group(): mixed.reshape(group_rows, feat_width) * gate_part]
  transfers between devices with their start and end apart: 6 -> 3, of which waited for: 1 -> 1; matrix products, arithmetic and copies ran while one was open for 2% -> 0% of each run, Pallas kernels for 0% -> 30%
where the time goes in v1:
time: 99.9 us; the launch traced here: 98.8 us
  Pallas kernels  59.9 us (60%)
  local copies, waits for them, and re-layouts  15.9 us (16%)
  waiting for transfers between devices  11.5 us (12%)
  starting transfers between devices  10.1 us (10%)
    pallas_call x4, Pallas kernels, run_tiles(): pl.pallas_call(functools.partial(block_kernel, kind, tile_of, count), gri...  59.9 us
    unnamed x34, local copies, waits for them, and re-layouts  15.2 us
    ppermute x3, waiting for transfers between devices, moved(): lax.ppermute(value, AXES, [(i, i + steps) for i in range(first, last)])  11.5 us
    ppermute x3, starting transfers between devices, moved(): lax.ppermute(value, AXES, [(i, i + steps) for i in range(first, last)])  10.1 us
  transfers between devices with their start and end apart: 3, of which 1 were waited for; matrix products, arithmetic and copies ran while one was open for 0% of the time, Pallas kernels for 30%

profile of v1, /device:TPU:9, one launch (start us, length us, event | category | flops | bytes accessed | tf_op | source)
XLA Modules:
  0.0 98.8 jit_solution(9293277515548966613)
XLA Ops:
  0.6 0.8 convert_element_type.3
  1.4 0.7 fusion
  2.2 3.5 %collective-permute-start = (bf16[80,128]{1,0:T(8,128)(2,1)S(1)}, bf16[80,128]{1,0:T(8,128)(2,1)S(1)}, u32[]{:S(2)}, u32[]{:S(2)}) collective-permute-start(bf16[80,128]{1,0:T(8,128)(2,1)S(1)} %pad_maximum_fusion), channel_id=1, source_target_pairs={{0,1},{1,2},{2,3},{3,4},{4,5},{5,6},{6,7},{7,8},{8,9},{9,10},{10,1... | collective-permute-start | bytes 61448 | tf_op jit(solution)/shard_map/ppermute | solution.py:283
  5.7 4.6 %collective-permute-start.1 = (bf16[80,128]{1,0:T(8,128)(2,1)S(1)}, bf16[80,128]{1,0:T(8,128)(2,1)S(1)}, u32[]{:S(2)}, u32[]{:S(2)}) collective-permute-start(bf16[80,128]{1,0:T(8,128)(2,1)S(1)} %pad_maximum_fusion.1), channel_id=1, source_target_pairs={{1,0},{2,1},{3,2},{4,3},{5,4},{6,5},{7,6},{8,7},{9,8},{10,9},{11,1... | collective-permute-start | bytes 61448 | tf_op jit(solution)/shard_map/ppermute | solution.py:283
  10.3 1.6 %copy-done = bf16[8192,128]{1,0:T(8,128)(2,1)S(1)} copy-done((bf16[8192,128]{1,0:T(8,128)(2,1)S(1)}, bf16[8192,128]{1,0:T(8,128)(2,1)}, u32[]{:S(2)}) %copy-start) | copy-done | bytes 2097176
  11.9 0.8 copy-done.3
  12.7 0.9 copy-done.4
  13.6 0.8 copy-done.5
  14.4 0.8 copy-done.6
  15.3 0.8 copy-done.7
  16.1 0.8 copy-done.8
  16.9 0.8 copy-done.9
  17.6 0.8 copy-done.10
  18.4 0.8 copy-done.11
  19.1 0.8 copy-done.12
  19.9 0.8 copy-done.13
  22.6 14.3 %shard_map.167 = (bf16[8192,128]{1,0:T(8,128)(2,1)}, f32[1152,512]{1,0:T(8,128)S(1)}) custom-call(s32[256]{0:T(256)S(1)} %copy-done.14, s32[8192]{0:T(1024)S(1)} %copy-done.3, bf16[8192,128]{1,0:T(8,128)(2,1)S(1)} %copy-done, bf16[8192,128]{1,0:T(8,128)(2,1)S(1)} %copy-done, bf16[8192,128]{1,0:T(8,128)(2,1)S(1)} %copy-done, bf16[8192,512]{1,0:T(8,128)(2,1)} %refs_5_.7, ...), custom_call_target="tpu_custom_call" | custom-call | flops 4096000000 | bytes 3276800 | tf_op jit(solution)/shard_map/pallas_call | solution.py:251
  36.9 1.4 %copy-done.1 = f32[1152,512]{1,0:T(8,128)} copy-done((f32[1152,512]{1,0:T(8,128)}, f32[1152,512]{1,0:T(8,128)S(1)}, u32[]{:S(2)}) %copy-start.1) | copy-done | bytes 2359320
  38.4 15.4 %shard_map.168 = (bf16[8192,128]{1,0:T(8,128)(2,1)}, f32[1152,512]{1,0:T(8,128)S(1)}, bf16[1024,512]{1,0:T(8,128)(2,1)S(1)}) custom-call(s32[256]{0:T(256)S(1)} %copy-done.14, s32[8192]{0:T(1024)S(1)} %copy-done.3, bf16[8192,128]{1,0:T(8,128)(2,1)S(1)} %copy-done, bf16[8192,128]{1,0:T(8,128)(2,1)S(1)} %copy-done, ...), custom_call_target="tpu_custom_call", output_to_operand_aliasing={{0}: (22, {})} | custom-call | flops 4096000000 | bytes 3276800 | tf_op jit(solution)/shard_map/pallas_call | solution.py:251
  53.8 1.4 %copy-done.2 = f32[1152,512]{1,0:T(8,128)} copy-done((f32[1152,512]{1,0:T(8,128)}, f32[1152,512]{1,0:T(8,128)S(1)}, u32[]{:S(2)}) %copy-start.2) | copy-done | bytes 2359320
  55.2 1.9 %collective-permute-start.2 = (bf16[1024,512]{1,0:T(8,128)(2,1)S(1)}, bf16[1024,512]{1,0:T(8,128)(2,1)S(1)}, u32[]{:S(2)}, u32[]{:S(2)}) collective-permute-start(bf16[1024,512]{1,0:T(8,128)(2,1)S(1)} %get-tuple-element.14), channel_id=1, source_target_pairs={{0,1},{1,2},{2,3},{3,4},{4,5},{5,6},{6,7},{7,8},{8,9},{9,10},{10,1... | collective-permute-start | bytes 3145736 | tf_op jit(solution)/shard_map/ppermute | solution.py:283
  57.2 15.1 %shard_map.169 = (bf16[8192,128]{1,0:T(8,128)(2,1)}, f32[1152,512]{1,0:T(8,128)S(1)}) custom-call(s32[256]{0:T(256)S(1)} %copy-done.14, s32[8192]{0:T(1024)S(1)} %copy-done.3, bf16[8192,128]{1,0:T(8,128)(2,1)S(1)} %copy-done, bf16[8192,128]{1,0:T(8,128)(2,1)S(1)} %copy-done, bf16[8192,128]{1,0:T(8,128)(2,1)S(1)} %copy-done, ...), custom_call_target="tpu_custom_call", output_to_operand_aliasing={{0}: (20, {})} | custom-call | flops 4096000000 | bytes 3276800 | tf_op jit(solution)/shard_map/pallas_call | solution.py:251
  72.3 11.5 %collective-permute-done.2.refs_22_ = bf16[1024,512]{1,0:T(8,128)(2,1)S(1)} collective-permute-done((bf16[1024,512]{1,0:T(8,128)(2,1)S(1)}, bf16[1024,512]{1,0:T(8,128)(2,1)S(1)}, u32[]{:S(2)}, u32[]{:S(2)}) %collective-permute-start.2) | collective-permute-done | bytes 1048608 | tf_op jit(solution)/shard_map/ppermute | solution.py:283
  83.8 15.0 %shard_map.170 = (bf16[8192,128]{1,0:T(8,128)(2,1)}, f32[1024,384]{1,0:T(8,128)}) custom-call(s32[256]{0:T(256)S(1)} %copy-done.14, s32[8192]{0:T(1024)S(1)} %copy-done.3, bf16[8192,128]{1,0:T(8,128)(2,1)S(1)} %copy-done, bf16[8192,128]{1,0:T(8,128)(2,1)S(1)} %copy-done, bf16[8192,128]{1,0:T(8,128)(2,1)S(1)} %copy-done, ...), custom_call_target="tpu_custom_call", output_to_operand_aliasing={{0}: (23, {})} | custom-call | flops 4096000000 | bytes 3276800 | tf_op jit(solution)/shard_map/pallas_call | solution.py:251
  (27 shorter events, 2.0 us)
Async XLA Ops:
  2.2 36.2 %collective-permute-start = (bf16[80,128]{1,0:T(8,128)(2,1)S(1)}, bf16[80,128]{1,0:T(8,128)(2,1)S(1)}, u32[]{:S(2)}, u32[]{:S(2)}) collective-permute-start(bf16[80,128]{1,0:T(8,128)(2,1)S(1)} %pad_maximum_fusion), channel_id=1, source_target_pairs={{0,1},{1,2},{2,3},{3,4},{4,5},{5,6},{6,7},{7,8},{8,9},{9,10},{10,1... | collective-permute-start | bytes 61448 | tf_op jit(solution)/shard_map/ppermute | solution.py:283
  5.7 32.6 %collective-permute-start.1 = (bf16[80,128]{1,0:T(8,128)(2,1)S(1)}, bf16[80,128]{1,0:T(8,128)(2,1)S(1)}, u32[]{:S(2)}, u32[]{:S(2)}) collective-permute-start(bf16[80,128]{1,0:T(8,128)(2,1)S(1)} %pad_maximum_fusion.1), channel_id=1, source_target_pairs={{1,0},{2,1},{3,2},{4,3},{5,4},{6,5},{7,6},{8,7},{9,8},{10,9},{11,1... | collective-permute-start | bytes 61448 | tf_op jit(solution)/shard_map/ppermute | solution.py:283
  10.3 1.6 %copy-start = (bf16[8192,128]{1,0:T(8,128)(2,1)S(1)}, bf16[8192,128]{1,0:T(8,128)(2,1)}, u32[]{:S(2)}) copy-start(bf16[8192,128]{1,0:T(8,128)(2,1)} %refs_4_.7) | copy-start | bytes 6291460
  11.9 0.8 copy-start.3
  12.7 0.9 copy-start.4
  13.6 0.8 copy-start.5
  14.4 0.8 copy-start.6
  15.3 0.8 copy-start.7
  16.1 0.8 copy-start.8
  16.9 0.8 copy-start.9
  17.6 0.8 copy-start.10
  18.4 0.8 copy-start.11
  19.1 0.8 copy-start.12
  19.9 0.8 copy-start.13
  20.7 0.7 copy-start.14
  21.3 0.7 copy-start.15
  22.0 0.7 copy-start.16
  36.9 1.4 %copy-start.1 = (f32[1152,512]{1,0:T(8,128)}, f32[1152,512]{1,0:T(8,128)S(1)}, u32[]{:S(2)}) copy-start(f32[1152,512]{1,0:T(8,128)S(1)} %get-tuple-element.9.refs_21_) | copy-start | bytes 7077892
  53.8 1.4 %copy-start.2 = (f32[1152,512]{1,0:T(8,128)}, f32[1152,512]{1,0:T(8,128)S(1)}, u32[]{:S(2)}) copy-start(f32[1152,512]{1,0:T(8,128)S(1)} %get-tuple-element.11.refs_19_) | copy-start | bytes 7077892
  55.2 28.6 %collective-permute-start.2 = (bf16[1024,512]{1,0:T(8,128)(2,1)S(1)}, bf16[1024,512]{1,0:T(8,128)(2,1)S(1)}, u32[]{:S(2)}, u32[]{:S(2)}) collective-permute-start(bf16[1024,512]{1,0:T(8,128)(2,1)S(1)} %get-tuple-element.14), channel_id=1, source_target_pairs={{0,1},{1,2},{2,3},{3,4},{4,5},{5,6},{6,7},{7,8},{8,9},{9,10},{10,1... | collective-permute-start | bytes 3145736 | tf_op jit(solution)/shard_map/ppermute | solution.py:283

commit v2 on v1

v2 whole, which is shorter than its diff:
```python
import functools
import math

import jax
import jax.numpy as jnp
from jax import lax
from jax.experimental import pallas as pl
from jax.experimental.pallas import tpu as pltpu
from jax.sharding import PartitionSpec as P

C_ATOM = 128
HEADS = 4
HEAD = C_ATOM // HEADS
C_TOKEN = 384
QUERY_BLOCK = 32
KEY_WINDOW = 128
ATOM_DEV = 8192
REACH = 64
TOK_DEV = 1024
DRIFT = 2048
EPSILON = 1e-05
MASKED = -1000000000.0
LIVE = 3e38

TILE = DRIFT
BLOCKS = TILE // QUERY_BLOCK
GROUP = 32
SPAN = TILE + 2 * REACH
TILES = ATOM_DEV // TILE
PART = 512
WIN = 128
ACC_ROWS = TOK_DEV + WIN
SUM_COLS = C_TOKEN + 128
PEN_OFF = 8
MASK_ROWS = ATOM_DEV // 128
PEN_ROWS = MASK_ROWS + 2 * PEN_OFF
QSCALE = 1.0 / math.sqrt(HEAD)

NT = (((1,), (1,)), ((), ()))
AXES = ("atom", "pair")
MESH = pl.DeviceIdType.MESH
VMEM_BYTES = 60 * 1024 * 1024


def dot(a, b):
    return jnp.dot(a, b, preferred_element_type=jnp.float32)


def layer_norm(rows, gain):
    same = lax.broadcasted_iota(jnp.int32, (C_ATOM, C_ATOM), 0) == lax.broadcasted_iota(
        jnp.int32, (C_ATOM, C_ATOM), 1
    )
    share = 1.0 / C_ATOM
    centering = jnp.where(same, 1.0 - share, -share).astype(jnp.bfloat16)
    center = dot(rows, centering)
    averaging = jnp.full((C_ATOM, C_ATOM), share, jnp.bfloat16)
    spread = dot((center * center).astype(jnp.bfloat16), averaging)
    return (center * lax.rsqrt(spread + EPSILON) * gain).astype(jnp.bfloat16)


def sigmoid(x):
    return 0.5 * jnp.tanh(0.5 * x) + 0.5


def tile_of(step):
    return jnp.where(step == 0, 1, jnp.where(step == 1, 3, jnp.where(step == 2, 2, 0)))


def here():
    return lax.axis_index("atom") * lax.axis_size("pair") + lax.axis_index("pair")


def place_of(device):
    pair = lax.axis_size("pair")
    return (device // pair, device % pair)


def attention_kernel(
    koff, cur, prev, nxt, bias, mask,
    g1, wq, wk, wv, wg, wo, g2, wfg, wfu, wfd,
    atoms_any, mask_any, marks_any,
    out, got_rows, got_marks,
    k_s, v_s, pen_s, q_s, gate_s, att_s, send_s, low, high, below, above,
    below_mask, above_mask, send_sem, recv_sem,
):
    step = pl.program_id(0)
    tile = tile_of(step)
    me = here()
    devices = lax.axis_size("atom") * lax.axis_size("pair")
    right = place_of((me + 1) % devices)
    left = place_of((me + devices - 1) % devices)

    def remote(source, target, n, device):
        return pltpu.make_async_remote_copy(
            src_ref=source,
            dst_ref=target,
            send_sem=send_sem.at[n],
            recv_sem=recv_sem.at[n],
            device_id=device,
            device_id_type=MESH,
        )

    edges = [
        remote(atoms_any.at[pl.ds(ATOM_DEV - REACH, REACH)], below, 0, right),
        remote(atoms_any.at[pl.ds(0, REACH)], above, 1, left),
        remote(mask_any.at[pl.ds(MASK_ROWS - 8, 8)], below_mask, 2, right),
        remote(mask_any.at[pl.ds(0, 8)], above_mask, 3, left),
    ]
    marks = remote(marks_any.at[pl.ds(MASK_ROWS - DRIFT // 128, DRIFT // 128)], got_marks, 4, right)
    tail = remote(send_s, got_rows, 5, right)

    @pl.when(step == 0)
    def _():
        barrier = pltpu.get_barrier_semaphore()
        for device in (left, right):
            pl.semaphore_signal(barrier, inc=1, device_id=device, device_id_type=MESH)
        pl.semaphore_wait(barrier, 2)
        for copy in edges:
            copy.start()
        marks.start()
        pen_s[PEN_OFF : PEN_OFF + MASK_ROWS, :] = jnp.where(mask[...] == 1, LIVE, MASKED)
        nothing = jnp.full((PEN_OFF, 128), MASKED, jnp.float32)
        pen_s[0:PEN_OFF, :] = nothing
        pen_s[PEN_ROWS - PEN_OFF :, :] = nothing
        low[...] = jnp.zeros((REACH, C_ATOM), jnp.bfloat16)
        high[...] = jnp.zeros((REACH, C_ATOM), jnp.bfloat16)

    @pl.when(step == 1)
    def _():
        for copy in edges:
            copy.wait()
        pen_s[0:PEN_OFF, :] = jnp.where((below_mask[...] == 1) & (me > 0), LIVE, MASKED)
        pen_s[PEN_ROWS - PEN_OFF :, :] = jnp.where(
            (above_mask[...] == 1) & (me < devices - 1), LIVE, MASKED
        )

        @pl.when(me > 0)
        def _():
            low[...] = below[...]

        @pl.when(me < devices - 1)
        def _():
            high[...] = above[...]

    first = jnp.where(tile == 0, low[...], prev[...])
    last = jnp.where(tile == TILES - 1, high[...], nxt[...])
    normed = layer_norm(jnp.concatenate([first, cur[...], last], axis=0), g1[...])
    kv = dot(normed, jnp.concatenate([wk[...], wv[...]], axis=1))
    k_s[...] = kv[:, :C_ATOM]
    v_s[...] = kv[:, C_ATOM:]
    qg = dot(normed[REACH : REACH + TILE], jnp.concatenate([wq[...], wg[...]], axis=1))
    q_s[...] = (qg[:, :C_ATOM] * QSCALE).astype(jnp.bfloat16)
    gate_s[...] = sigmoid(qg[:, C_ATOM:])

    lane = lax.broadcasted_iota(jnp.int32, (1, C_ATOM), 1)
    heads = [(lane // HEAD == h) for h in range(HEADS)]
    head_ones = [m.astype(jnp.bfloat16) for m in heads]
    eye = (
        lax.broadcasted_iota(jnp.int32, (KEY_WINDOW, KEY_WINDOW), 0)
        == lax.broadcasted_iota(jnp.int32, (KEY_WINDOW, KEY_WINDOW), 1)
    ).astype(jnp.bfloat16)
    ones = jnp.ones((KEY_WINDOW, 128), jnp.bfloat16)

    def group(g, carry):
        g0 = pl.multiple_of(g * (GROUP * QUERY_BLOCK), GROUP * QUERY_BLOCK)
        scores, limits, weights, mixes = [], [], [], []
        offs = [
            jnp.clip(koff[tile * BLOCKS + g * GROUP + blk], -REACH, -QUERY_BLOCK)
            for blk in range(GROUP)
        ]
        rows = [pl.ds(g0 + blk * QUERY_BLOCK, QUERY_BLOCK) for blk in range(GROUP)]
        windows = [
            pl.ds(g0 + (blk * QUERY_BLOCK + REACH) + offs[blk], KEY_WINDOW) for blk in range(GROUP)
        ]
        for blk in range(GROUP):
            keys = k_s[windows[blk], :].astype(jnp.bfloat16)
            q = q_s[rows[blk], :]
            stacked = jnp.concatenate([q * m for m in head_ones], axis=0)
            biases = jnp.concatenate(
                [
                    bias[rows[blk], h * KEY_WINDOW : (h + 1) * KEY_WINDOW]
                    for h in range(HEADS)
                ],
                axis=0,
            )
            scores.append(
                lax.dot_general(
                    jnp.concatenate([stacked, biases], axis=1),
                    jnp.concatenate([keys, eye], axis=1),
                    NT,
                    preferred_element_type=jnp.float32,
                )
            )
            place = tile * TILE + g0 + (blk * QUERY_BLOCK + PEN_OFF * 128) + offs[blk]
            turn = 128 - (place & 127)
            pair = pen_s[pl.ds(place >> 7, 2), :]
            turned = pltpu.roll(pair, turn & 127, 1)
            limits.append(jnp.where(lane < turn, turned[0:1], turned[1:2]))
        for blk in range(GROUP):
            held = jnp.minimum(scores[blk], limits[blk])
            top = jnp.max(held, axis=1, keepdims=True)
            weights.append(jnp.exp(held - top).astype(jnp.bfloat16))
        for blk in range(GROUP):
            values = v_s[windows[blk], :].astype(jnp.bfloat16)
            mixes.append(dot(weights[blk], jnp.concatenate([values, ones], axis=1)))
        for blk in range(GROUP):
            mixed = mixes[blk]
            num = mixed[0:QUERY_BLOCK, :C_ATOM]
            den = mixed[0:QUERY_BLOCK, C_ATOM:]
            for h in range(1, HEADS):
                part = mixed[h * QUERY_BLOCK : (h + 1) * QUERY_BLOCK]
                num = jnp.where(heads[h], part[:, :C_ATOM], num)
                den = jnp.where(heads[h], part[:, C_ATOM:], den)
            att_s[rows[blk], :] = (num / den * gate_s[rows[blk], :]).astype(jnp.bfloat16)
        return carry

    lax.fori_loop(0, BLOCKS // GROUP, group, 0)

    updated = (cur[...].astype(jnp.float32) + dot(att_s[...], wo[...])).astype(jnp.bfloat16)
    second = layer_norm(updated, g2[...])
    gated = dot(second, wfg[...])
    hidden = (gated * sigmoid(gated) * dot(second, wfu[...])).astype(jnp.bfloat16)
    atom_out = (updated.astype(jnp.float32) + dot(hidden, wfd[...])).astype(jnp.bfloat16)
    out[...] = atom_out

    @pl.when(step == 1)
    def _():
        send_s[...] = out[...]
        tail.start()

    @pl.when(step == TILES - 1)
    def _():
        marks.wait()
        tail.wait()


def attend(key_offsets, atoms, pair_bias, mask2, marks, weights):
    per = TILE // REACH
    blocks = ATOM_DEV // REACH
    whole = lambda shape: pl.BlockSpec(shape, lambda t: (0,) * len(shape))
    anywhere = pl.BlockSpec(memory_space=pl.ANY)
    tiles = lambda width: pl.BlockSpec((TILE, width), lambda t: (tile_of(t), 0))
    in_specs = [
        pl.BlockSpec(memory_space=pltpu.SMEM),
        tiles(C_ATOM),
        pl.BlockSpec((REACH, C_ATOM), lambda t: (jnp.maximum(tile_of(t) * per - 1, 0), 0)),
        pl.BlockSpec((REACH, C_ATOM), lambda t: (jnp.minimum(tile_of(t) * per + per, blocks - 1), 0)),
        tiles(HEADS * KEY_WINDOW),
        whole(mask2.shape),
        *[whole(w.shape) for w in weights],
        anywhere,
        anywhere,
        anywhere,
    ]
    mark_rows = DRIFT // 128
    return pl.pallas_call(
        attention_kernel,
        grid=(TILES,),
        in_specs=in_specs,
        out_specs=[tiles(C_ATOM), anywhere, anywhere],
        out_shape=[
            jax.ShapeDtypeStruct((ATOM_DEV, C_ATOM), jnp.bfloat16),
            jax.ShapeDtypeStruct((DRIFT, C_ATOM), jnp.bfloat16),
            jax.ShapeDtypeStruct((mark_rows, 128), jnp.int32),
        ],
        scratch_shapes=[
            pltpu.VMEM((SPAN, C_ATOM), jnp.float32),
            pltpu.VMEM((SPAN, C_ATOM), jnp.float32),
            pltpu.VMEM((PEN_ROWS, 128), jnp.float32),
            pltpu.VMEM((TILE, C_ATOM), jnp.bfloat16),
            pltpu.VMEM((TILE, C_ATOM), jnp.float32),
            pltpu.VMEM((TILE, C_ATOM), jnp.bfloat16),
            pltpu.VMEM((DRIFT, C_ATOM), jnp.bfloat16),
            *[pltpu.VMEM((REACH, C_ATOM), jnp.bfloat16) for _ in range(4)],
            pltpu.VMEM((8, 128), jnp.int32),
            pltpu.VMEM((8, 128), jnp.int32),
            pltpu.SemaphoreType.DMA((6,)),
            pltpu.SemaphoreType.DMA((6,)),
        ],
        compiler_params=pltpu.CompilerParams(
            dimension_semantics=("arbitrary",),
            vmem_limit_bytes=VMEM_BYTES,
            collective_id=0,
            has_side_effects=True,
        ),
        cost_estimate=pl.CostEstimate(
            flops=6 * 10**9, bytes_accessed=14 * 2**20, transcendentals=6 * 10**6
        ),
    )(key_offsets, atoms, atoms, atoms, pair_bias, mask2, *weights, atoms, mask2, marks)


def pool_kernel(tok, far_tok, rows, far_rows, marks, far_marks, wp, out, pooled, proj_s, acc_s):
    step = pl.program_id(0)
    base = here() * TOK_DEV

    @pl.when(step == 0)
    def _():
        proj_s[:, C_TOKEN:] = jnp.ones((TILE, 128), jnp.bfloat16)
        acc_s[...] = jnp.zeros(acc_s.shape, jnp.float32)

    def add_tile(values, mark_of, mark_row):
        proj_s[:, :C_TOKEN] = jnp.maximum(dot(values, wp[...]), 0.0).astype(jnp.bfloat16)
        slots = lax.broadcasted_iota(jnp.int32, (WIN, PART), 0)
        parts = []
        for part in range(TILE // PART):
            mark = mark_row(part)
            local = jnp.where(mark & 1 == 1, (mark >> 1) - base, -1)
            row = jnp.concatenate([local[i : i + 1] for i in range(PART // 128)], axis=1)
            start = jnp.clip((((mark_of(part * PART) >> 1) - base) >> 3) << 3, 0, TOK_DEV)
            end = jnp.minimum((mark_of(part * PART + PART - 1) >> 1) - base, TOK_DEV - 1)
            parts.append((row, start, (jnp.maximum(end - start, 0) >> 7) + 1))

        def window_sums(part, i):
            row, start, _ = parts[part]
            at = pl.multiple_of(start + i * WIN, 8)
            table = (row - at == slots).astype(jnp.bfloat16)
            return at, dot(table, proj_s[part * PART : (part + 1) * PART, :])

        for at, sums in [window_sums(part, 0) for part in range(len(parts))]:
            acc_s[pl.ds(at, WIN), :] += sums
        most = parts[0][2]
        for _, _, n in parts[1:]:
            most = jnp.maximum(most, n)

        @pl.when(most > 1)
        def _():
            for part in range(len(parts)):

                def add(i, carry, part=part):
                    at, sums = window_sums(part, i)
                    acc_s[pl.ds(at, WIN), :] += sums
                    return carry

                lax.fori_loop(1, parts[part][2], add, 0)

    per = PART // 128

    @pl.when(step < TILES)
    def _():
        out[...] = rows[...]
        add_tile(
            rows[...],
            lambda a: tok[step * TILE + a],
            lambda part: marks[pl.ds(step * (TILE // 128) + part * per, per), :],
        )

    @pl.when(step == TILES)
    def _():
        add_tile(
            far_rows[...],
            lambda a: far_tok[a],
            lambda part: far_marks[part * per : (part + 1) * per, :],
        )
        counts = jnp.maximum(acc_s[0:TOK_DEV, C_TOKEN:], 1.0)
        pooled[...] = acc_s[0:TOK_DEV, :C_TOKEN] / jnp.concatenate(
            [counts] * (C_TOKEN // 128), axis=1
        )


def pool(marks, far_marks, rows, far_rows, w_pool):
    whole = lambda shape: pl.BlockSpec(shape, lambda t, *_: (0,) * len(shape))
    tiles = pl.BlockSpec((TILE, C_ATOM), lambda t, *_: (jnp.minimum(t, TILES - 1), 0))
    return pl.pallas_call(
        pool_kernel,
        grid_spec=pltpu.PrefetchScalarGridSpec(
            num_scalar_prefetch=2,
            grid=(TILES + 1,),
            in_specs=[
                tiles,
                whole(far_rows.shape),
                whole(marks.shape),
                whole(far_marks.shape),
                whole(w_pool.shape),
            ],
            out_specs=[tiles, whole((TOK_DEV, C_TOKEN))],
            scratch_shapes=[
                pltpu.VMEM((TILE, SUM_COLS), jnp.bfloat16),
                pltpu.VMEM((ACC_ROWS, SUM_COLS), jnp.float32),
            ],
        ),
        out_shape=[
            jax.ShapeDtypeStruct((ATOM_DEV, C_ATOM), jnp.bfloat16),
            jax.ShapeDtypeStruct((TOK_DEV, C_TOKEN), jnp.float32),
        ],
        compiler_params=pltpu.CompilerParams(
            dimension_semantics=("arbitrary",), vmem_limit_bytes=VMEM_BYTES
        ),
        cost_estimate=pl.CostEstimate(
            flops=5 * 10**9, bytes_accessed=8 * 2**20, transcendentals=0
        ),
    )(marks.reshape(-1), far_marks.reshape(-1), rows, far_rows, marks, far_marks, w_pool)


def shards(
    atoms,
    pair_bias,
    key_offsets,
    atom_mask,
    atom_token,
    norm_gain,
    w_query,
    w_key,
    w_value,
    w_gate,
    w_out,
    trans_gain,
    w_ff_gate,
    w_ff_up,
    w_ff_down,
    w_pool,
):
    mask2 = atom_mask.reshape(MASK_ROWS, 128)
    marks = atom_token.reshape(MASK_ROWS, 128) * 2 + mask2
    weights = (
        norm_gain[None],
        w_query,
        w_key,
        w_value,
        w_gate,
        w_out,
        trans_gain[None],
        w_ff_gate,
        w_ff_up,
        w_ff_down,
    )
    rows, far_rows, far_marks = attend(key_offsets, atoms, pair_bias, mask2, marks, weights)
    return tuple(pool(marks, far_marks, rows, far_rows, w_pool))


def solution(mesh):
    rows = P(("atom", "pair"))
    wide = P(("atom", "pair"), None)
    in_specs = (wide, wide, rows, rows, rows) + (P(),) * 11
    return jax.shard_map(
        shards, mesh=mesh, in_specs=in_specs, out_specs=(wide, wide), check_vma=False
    )
```

time: 99.9 us -> 47.5 us (0.48)
  the two profiles are of different devices: /device:TPU:9 before, /device:TPU:0 now
where the time goes in v2:
time: 47.5 us; the launch traced here: 47.1 us
  Pallas kernels  43.7 us (92%)
  other arithmetic  2.77 us (6%)
  between operations  0.64 us (1%)
    pallas_call x1, Pallas kernels, attend(): pl.pallas_call(attention_kernel, grid=(TILES,), in_specs=in_specs, out_sp...  34.6 us
    pallas_call x1, Pallas kernels, pool(): pl.pallas_call(pool_kernel, grid_spec=pltpu.PrefetchScalarGridSpec(num_sc...  9.1 us
    add x2, other arithmetic, shards(): marks = atom_token.reshape(MASK_ROWS, 128) * 2 + mask2  2.77 us

profile of v2, /device:TPU:0, one launch (start us, length us, event | category | flops | bytes accessed | tf_op | source)
XLA Modules:
  0.0 47.1 jit_solution(4089476888567529157)
XLA Ops:
  0.6 1.4 %bitcast_add_fusion.marks_any.marks = s32[64,128]{1,0:T(8,128)} fusion(s32[8192]{0:T(1024)} %param.20, s32[8192]{0:T(1024)} %param.19), kind=kLoop, calls=%fused_computation | loop fusion | flops 16384 | bytes 98304 | tf_op jit(solution)/shard_map/add | solution.py:413
  2.0 1.4 %multiply_add_fusion.tok = s32[8192]{0:T(1024)} fusion(s32[8192]{0:T(1024)} %param.19, s32[8192]{0:T(1024)} %param.20), kind=kLoop, calls=%fused_computation.1 | loop fusion | flops 16384 | bytes 98304 | tf_op jit(solution)/shard_map/add | solution.py:413
  3.4 34.6 %shard_map.167 = (bf16[8192,128]{1,0:T(8,128)(2,1)}, bf16[2048,128]{1,0:T(8,128)(2,1)}, s32[16,128]{1,0:T(8,128)}) custom-call(s32[256]{0:T(256)} %koff.1, bf16[8192,128]{1,0:T(8,128)(2,1)} %atoms_any.1, bf16[8192,128]{1,0:T(8,128)(2,1)} %atoms_any.1, bf16[8192,128]{1,0:T(8,128)(2,1)} %atoms_any.1, bf16[8192,512]{1,0:T(8,128)(2,1)} %bias.1, ...), custom_call_target="tpu_custom_call" | custom-call | flops 6000000000 | bytes 14680064 | tf_op jit(solution)/shard_map/pallas_call | solution.py:256
  38.0 9.1 %shard_map.168 = (bf16[8192,128]{1,0:T(8,128)(2,1)}, f32[1024,384]{1,0:T(8,128)}) custom-call(s32[8192]{0:T(1024)} %multiply_add_fusion.tok, s32[2048]{0:T(1024)} %bitcast.11, bf16[8192,128]{1,0:T(8,128)(2,1)} %get-tuple-element.6.rows, bf16[2048,128]{1,0:T(8,128)(2,1)} %get-tuple-element.7.far_rows, s32[64,128]{1,0:T(8,128)} %bitcast_add_fusion.marks_any.marks, ...), custom_call_target="tpu_custom_call" | custom-call | flops 5000000000 | bytes 8388608 | tf_op jit(solution)/shard_map/pallas_call | solution.py:363

commit v3 on v2

v3 whole, which is shorter than its diff:
```python
import functools
import math

import jax
import jax.numpy as jnp
from jax import lax
from jax.experimental import pallas as pl
from jax.experimental.pallas import tpu as pltpu
from jax.sharding import PartitionSpec as P

C_ATOM = 128
HEADS = 4
HEAD = C_ATOM // HEADS
C_TOKEN = 384
QUERY_BLOCK = 32
KEY_WINDOW = 128
ATOM_DEV = 8192
REACH = 64
TOK_DEV = 1024
DRIFT = 2048
EPSILON = 1e-05
MASKED = -1000000000.0
LIVE = 3e38

TILE = DRIFT
BLOCKS = TILE // QUERY_BLOCK
SPAN = TILE + 2 * REACH
TILES = ATOM_DEV // TILE
PART = 512
WIN = 128
ACC_ROWS = TOK_DEV + WIN
SUM_COLS = C_TOKEN + 128
PEN_OFF = 8
MASK_ROWS = ATOM_DEV // 128
FAR = DRIFT // 128
PEN_ROWS = MASK_ROWS + 2 * PEN_OFF
QSCALE = 1.0 / math.sqrt(HEAD)

NT = (((1,), (1,)), ((), ()))
AXES = ("atom", "pair")
MESH = pl.DeviceIdType.MESH
VMEM_BYTES = 60 * 1024 * 1024


def dot(a, b):
    return jnp.dot(a, b, preferred_element_type=jnp.float32)


def layer_norm(rows, gain):
    same = lax.broadcasted_iota(jnp.int32, (C_ATOM, C_ATOM), 0) == lax.broadcasted_iota(
        jnp.int32, (C_ATOM, C_ATOM), 1
    )
    share = 1.0 / C_ATOM
    centering = jnp.where(same, 1.0 - share, -share).astype(jnp.bfloat16)
    center = dot(rows, centering)
    averaging = jnp.full((C_ATOM, C_ATOM), share, jnp.bfloat16)
    spread = dot((center * center).astype(jnp.bfloat16), averaging)
    return (center * lax.rsqrt(spread + EPSILON) * gain).astype(jnp.bfloat16)


def sigmoid(x):
    return 0.5 * jnp.tanh(0.5 * x) + 0.5


def tile_of(step):
    return jnp.where(step == 0, 1, jnp.where(step == 1, 3, jnp.where(step == 2, 2, 0)))


def here():
    return lax.axis_index("atom") * lax.axis_size("pair") + lax.axis_index("pair")


def place_of(device):
    pair = lax.axis_size("pair")
    return (device // pair, device % pair)


def attention_kernel(
    koff, cur, prev, nxt, bias, mask, ids,
    g1, wq, wk, wv, wg, wo, g2, wfg, wfu, wfd,
    atoms_any, mask_any,
    out, got_rows, got_marks,
    k_s, v_s, pen_s, q_s, gate_s, att_s, send_s, low, high, below, above,
    below_mask, above_mask, marks_s, send_sem, recv_sem,
):
    step = pl.program_id(0)
    tile = tile_of(step)
    me = here()
    devices = lax.axis_size("atom") * lax.axis_size("pair")
    right = place_of((me + 1) % devices)
    left = place_of((me + devices - 1) % devices)

    def remote(source, target, n, device):
        return pltpu.make_async_remote_copy(
            src_ref=source,
            dst_ref=target,
            send_sem=send_sem.at[n],
            recv_sem=recv_sem.at[n],
            device_id=device,
            device_id_type=MESH,
        )

    ups = [
        remote(atoms_any.at[pl.ds(ATOM_DEV - REACH, REACH)], below, 0, right),
        remote(mask_any.at[pl.ds(MASK_ROWS - 8, 8)], below_mask, 2, right),
    ]
    downs = [
        remote(atoms_any.at[pl.ds(0, REACH)], above, 1, left),
        remote(mask_any.at[pl.ds(0, 8)], above_mask, 3, left),
    ]
    tails = [remote(marks_s, got_marks, 4, right), remote(send_s, got_rows, 5, right)]
    has_right, has_left = me < devices - 1, me > 0

    @pl.when(step == 0)
    def _():
        barrier = pltpu.get_barrier_semaphore()

        @pl.when(has_right)
        def _():
            pl.semaphore_signal(barrier, inc=1, device_id=right, device_id_type=MESH)

        @pl.when(has_left)
        def _():
            pl.semaphore_signal(barrier, inc=1, device_id=left, device_id_type=MESH)

        pen_s[PEN_OFF : PEN_OFF + MASK_ROWS, :] = jnp.where(mask[...] == 1, LIVE, MASKED)
        nothing = jnp.full((PEN_OFF, 128), MASKED, jnp.float32)
        pen_s[0:PEN_OFF, :] = nothing
        pen_s[PEN_ROWS - PEN_OFF :, :] = nothing
        low[...] = jnp.zeros((REACH, C_ATOM), jnp.bfloat16)
        high[...] = jnp.zeros((REACH, C_ATOM), jnp.bfloat16)
        marks_s[...] = ids[...] * 2 + mask[MASK_ROWS - FAR :, :]

    @pl.when(step == 1)
    def _():
        @pl.when(has_left)
        def _():
            for copy in ups:
                copy.wait_recv()
            low[...] = below[...]
            pen_s[0:PEN_OFF, :] = jnp.where(below_mask[...] == 1, LIVE, MASKED)
            for copy in downs:
                copy.wait_send()

        @pl.when(has_right)
        def _():
            for copy in downs:
                copy.wait_recv()
            high[...] = above[...]
            pen_s[PEN_ROWS - PEN_OFF :, :] = jnp.where(above_mask[...] == 1, LIVE, MASKED)
            for copy in ups:
                copy.wait_send()

    first = jnp.where(tile == 0, low[...], prev[...])
    last = jnp.where(tile == TILES - 1, high[...], nxt[...])
    normed = layer_norm(jnp.concatenate([first, cur[...], last], axis=0), g1[...])
    kv = dot(normed, jnp.concatenate([wk[...], wv[...]], axis=1))
    k_s[...] = kv[:, :C_ATOM]
    v_s[...] = kv[:, C_ATOM:]
    qg = dot(normed[REACH : REACH + TILE], jnp.concatenate([wq[...], wg[...]], axis=1))
    q_s[...] = (qg[:, :C_ATOM] * QSCALE).astype(jnp.bfloat16)
    gate_s[...] = sigmoid(qg[:, C_ATOM:])

    @pl.when(step == 0)
    def _():
        barrier = pltpu.get_barrier_semaphore()
        pl.semaphore_wait(barrier, has_right.astype(jnp.int32) + has_left.astype(jnp.int32))

        @pl.when(has_right)
        def _():
            for copy in ups:
                copy.start()
            tails[0].start()

        @pl.when(has_left)
        def _():
            for copy in downs:
                copy.start()

    lane = lax.broadcasted_iota(jnp.int32, (1, C_ATOM), 1)
    heads = [(lane // HEAD == h) for h in range(HEADS)]
    head_ones = [m.astype(jnp.bfloat16) for m in heads]
    eye = (
        lax.broadcasted_iota(jnp.int32, (KEY_WINDOW, KEY_WINDOW), 0)
        == lax.broadcasted_iota(jnp.int32, (KEY_WINDOW, KEY_WINDOW), 1)
    ).astype(jnp.bfloat16)
    ones = jnp.ones((KEY_WINDOW, 128), jnp.bfloat16)

    offs = [
        jnp.clip(koff[tile * BLOCKS + blk], -REACH, -QUERY_BLOCK) for blk in range(BLOCKS)
    ]
    rows = [slice(blk * QUERY_BLOCK, (blk + 1) * QUERY_BLOCK) for blk in range(BLOCKS)]
    windows = [
        pl.ds(blk * QUERY_BLOCK + REACH + offs[blk], KEY_WINDOW) for blk in range(BLOCKS)
    ]
    scores, limits, weights, mixes = {}, {}, {}, {}

    def score(blk):
        keys = k_s[windows[blk], :].astype(jnp.bfloat16)
        q = q_s[rows[blk], :]
        stacked = jnp.concatenate([q * m for m in head_ones], axis=0)
        biases = jnp.concatenate(
            [
                bias[rows[blk], h * KEY_WINDOW : (h + 1) * KEY_WINDOW]
                for h in range(HEADS)
            ],
            axis=0,
        )
        scores[blk] = lax.dot_general(
            jnp.concatenate([stacked, biases], axis=1),
            jnp.concatenate([keys, eye], axis=1),
            NT,
            preferred_element_type=jnp.float32,
        )
        place = tile * TILE + (blk * QUERY_BLOCK + PEN_OFF * 128) + offs[blk]
        turn = 128 - (place & 127)
        pair = pen_s[pl.ds(place >> 7, 2), :]
        turned = pltpu.roll(pair, turn & 127, 1)
        limits[blk] = jnp.where(lane < turn, turned[0:1], turned[1:2])

    def soften(blk):
        held = jnp.minimum(scores.pop(blk), limits.pop(blk))
        top = jnp.max(held, axis=1, keepdims=True)
        weights[blk] = jnp.exp(held - top).astype(jnp.bfloat16)

    def mix(blk):
        values = v_s[windows[blk], :].astype(jnp.bfloat16)
        mixes[blk] = dot(weights.pop(blk), jnp.concatenate([values, ones], axis=1))

    def finish(blk):
        mixed = mixes.pop(blk)
        num = mixed[0:QUERY_BLOCK, :C_ATOM]
        den = mixed[0:QUERY_BLOCK, C_ATOM:]
        for h in range(1, HEADS):
            part = mixed[h * QUERY_BLOCK : (h + 1) * QUERY_BLOCK]
            num = jnp.where(heads[h], part[:, :C_ATOM], num)
            den = jnp.where(heads[h], part[:, C_ATOM:], den)
        att_s[rows[blk], :] = (num / den * gate_s[rows[blk], :]).astype(jnp.bfloat16)

    for stage in (score, soften, mix, finish):
        for blk in range(BLOCKS):
            stage(blk)

    updated = (cur[...].astype(jnp.float32) + dot(att_s[...], wo[...])).astype(jnp.bfloat16)
    second = layer_norm(updated, g2[...])
    gated = dot(second, wfg[...])
    hidden = (gated * sigmoid(gated) * dot(second, wfu[...])).astype(jnp.bfloat16)
    atom_out = (updated.astype(jnp.float32) + dot(hidden, wfd[...])).astype(jnp.bfloat16)
    out[...] = atom_out

    @pl.when((step == 1) & has_right)
    def _():
        send_s[...] = out[...]
        tails[1].start()

    @pl.when((step == TILES - 1) & has_right)
    def _():
        for copy in tails:
            copy.wait_send()

    @pl.when((step == TILES - 1) & has_left)
    def _():
        for copy in tails:
            copy.wait_recv()


def attend(key_offsets, atoms, pair_bias, mask2, ids2, weights):
    per = TILE // REACH
    blocks = ATOM_DEV // REACH
    whole = lambda shape: pl.BlockSpec(shape, lambda t: (0,) * len(shape))
    anywhere = pl.BlockSpec(memory_space=pl.ANY)
    tiles = lambda width: pl.BlockSpec((TILE, width), lambda t: (tile_of(t), 0))
    in_specs = [
        pl.BlockSpec(memory_space=pltpu.SMEM),
        tiles(C_ATOM),
        pl.BlockSpec((REACH, C_ATOM), lambda t: (jnp.maximum(tile_of(t) * per - 1, 0), 0)),
        pl.BlockSpec((REACH, C_ATOM), lambda t: (jnp.minimum(tile_of(t) * per + per, blocks - 1), 0)),
        tiles(HEADS * KEY_WINDOW),
        whole(mask2.shape),
        pl.BlockSpec((FAR, 128), lambda t: (MASK_ROWS // FAR - 1, 0)),
        *[whole(w.shape) for w in weights],
        anywhere,
        anywhere,
    ]
    return pl.pallas_call(
        attention_kernel,
        grid=(TILES,),
        in_specs=in_specs,
        out_specs=[tiles(C_ATOM), anywhere, anywhere],
        out_shape=[
            jax.ShapeDtypeStruct((ATOM_DEV, C_ATOM), jnp.bfloat16),
            jax.ShapeDtypeStruct((DRIFT, C_ATOM), jnp.bfloat16),
            jax.ShapeDtypeStruct((FAR, 128), jnp.int32),
        ],
        scratch_shapes=[
            pltpu.VMEM((SPAN, C_ATOM), jnp.float32),
            pltpu.VMEM((SPAN, C_ATOM), jnp.float32),
            pltpu.VMEM((PEN_ROWS, 128), jnp.float32),
            pltpu.VMEM((TILE, C_ATOM), jnp.bfloat16),
            pltpu.VMEM((TILE, C_ATOM), jnp.float32),
            pltpu.VMEM((TILE, C_ATOM), jnp.bfloat16),
            pltpu.VMEM((DRIFT, C_ATOM), jnp.bfloat16),
            *[pltpu.VMEM((REACH, C_ATOM), jnp.bfloat16) for _ in range(4)],
            pltpu.VMEM((8, 128), jnp.int32),
            pltpu.VMEM((8, 128), jnp.int32),
            pltpu.VMEM((FAR, 128), jnp.int32),
            pltpu.SemaphoreType.DMA((6,)),
            pltpu.SemaphoreType.DMA((6,)),
        ],
        compiler_params=pltpu.CompilerParams(
            dimension_semantics=("arbitrary",),
            vmem_limit_bytes=VMEM_BYTES,
            collective_id=0,
            has_side_effects=True,
        ),
        cost_estimate=pl.CostEstimate(
            flops=6 * 10**9, bytes_accessed=14 * 2**20, transcendentals=6 * 10**6
        ),
    )(key_offsets, atoms, atoms, atoms, pair_bias, mask2, ids2, *weights, atoms, mask2)


def pool_kernel(
    tok, far_tok, rows, far_rows, ids, mask, far_marks, wp, out, pooled, proj_s, acc_s
):
    step = pl.program_id(0)
    me = here()
    base = me * TOK_DEV

    @pl.when(step == 0)
    def _():
        proj_s[:, C_TOKEN:] = jnp.ones((TILE, 128), jnp.bfloat16)
        acc_s[...] = jnp.zeros(acc_s.shape, jnp.float32)

    def add_tile(values, token_of, local_of):
        proj_s[:, :C_TOKEN] = jnp.maximum(dot(values, wp[...]), 0.0).astype(jnp.bfloat16)
        slots = lax.broadcasted_iota(jnp.int32, (WIN, PART), 0)
        parts = []
        for part in range(TILE // PART):
            local = local_of(part)
            row = jnp.concatenate([local[i : i + 1] for i in range(PART // 128)], axis=1)
            start = jnp.clip(((token_of(part * PART) - base) >> 3) << 3, 0, TOK_DEV)
            end = jnp.minimum(token_of(part * PART + PART - 1) - base, TOK_DEV - 1)
            parts.append((row, start, (jnp.maximum(end - start, 0) >> 7) + 1))

        def window_sums(part, i):
            row, start, _ = parts[part]
            at = pl.multiple_of(start + i * WIN, 8)
            table = (row - at == slots).astype(jnp.bfloat16)
            return at, dot(table, proj_s[part * PART : (part + 1) * PART, :])

        for at, sums in [window_sums(part, 0) for part in range(len(parts))]:
            acc_s[pl.ds(at, WIN), :] += sums
        most = parts[0][2]
        for _, _, n in parts[1:]:
            most = jnp.maximum(most, n)

        @pl.when(most > 1)
        def _():
            for part in range(len(parts)):

                def add(i, carry, part=part):
                    at, sums = window_sums(part, i)
                    acc_s[pl.ds(at, WIN), :] += sums
                    return carry

                lax.fori_loop(1, parts[part][2], add, 0)

    per = PART // 128

    @pl.when(step < TILES)
    def _():
        def local_of(part):
            at = pl.ds(step * (TILE // 128) + part * per, per)
            return jnp.where(mask[at, :] == 1, ids[at, :] - base, -1)

        out[...] = rows[...]
        add_tile(rows[...], lambda a: tok[step * TILE + a], local_of)

    @pl.when((step == TILES) & (me > 0))
    def _():
        def local_of(part):
            mark = far_marks[part * per : (part + 1) * per, :]
            return jnp.where(mark & 1 == 1, (mark >> 1) - base, -1)

        add_tile(far_rows[...], lambda a: far_tok[a] >> 1, local_of)

    @pl.when(step == TILES)
    def _():
        counts = jnp.maximum(acc_s[0:TOK_DEV, C_TOKEN:], 1.0)
        pooled[...] = acc_s[0:TOK_DEV, :C_TOKEN] / jnp.concatenate(
            [counts] * (C_TOKEN // 128), axis=1
        )


def pool(tokens, ids2, mask2, far_marks, rows, far_rows, w_pool):
    whole = lambda shape: pl.BlockSpec(shape, lambda t, *_: (0,) * len(shape))
    tiles = pl.BlockSpec((TILE, C_ATOM), lambda t, *_: (jnp.minimum(t, TILES - 1), 0))
    return pl.pallas_call(
        pool_kernel,
        grid_spec=pltpu.PrefetchScalarGridSpec(
            num_scalar_prefetch=2,
            grid=(TILES + 1,),
            in_specs=[
                tiles,
                whole(far_rows.shape),
                whole(ids2.shape),
                whole(mask2.shape),
                whole(far_marks.shape),
                whole(w_pool.shape),
            ],
            out_specs=[tiles, whole((TOK_DEV, C_TOKEN))],
            scratch_shapes=[
                pltpu.VMEM((TILE, SUM_COLS), jnp.bfloat16),
                pltpu.VMEM((ACC_ROWS, SUM_COLS), jnp.float32),
            ],
        ),
        out_shape=[
            jax.ShapeDtypeStruct((ATOM_DEV, C_ATOM), jnp.bfloat16),
            jax.ShapeDtypeStruct((TOK_DEV, C_TOKEN), jnp.float32),
        ],
        compiler_params=pltpu.CompilerParams(
            dimension_semantics=("arbitrary",), vmem_limit_bytes=VMEM_BYTES
        ),
        cost_estimate=pl.CostEstimate(
            flops=5 * 10**9, bytes_accessed=8 * 2**20, transcendentals=0
        ),
    )(tokens, far_marks.reshape(-1), rows, far_rows, ids2, mask2, far_marks, w_pool)


def shards(
    atoms,
    pair_bias,
    key_offsets,
    atom_mask,
    atom_token,
    norm_gain,
    w_query,
    w_key,
    w_value,
    w_gate,
    w_out,
    trans_gain,
    w_ff_gate,
    w_ff_up,
    w_ff_down,
    w_pool,
):
    mask2 = atom_mask.reshape(MASK_ROWS, 128)
    ids2 = atom_token.reshape(MASK_ROWS, 128)
    weights = (
        norm_gain[None],
        w_query,
        w_key,
        w_value,
        w_gate,
        w_out,
        trans_gain[None],
        w_ff_gate,
        w_ff_up,
        w_ff_down,
    )
    rows, far_rows, far_marks = attend(key_offsets, atoms, pair_bias, mask2, ids2, weights)
    return tuple(pool(atom_token, ids2, mask2, far_marks, rows, far_rows, w_pool))


def solution(mesh):
    rows = P(("atom", "pair"))
    wide = P(("atom", "pair"), None)
    in_specs = (wide, wide, rows, rows, rows) + (P(),) * 11
    return jax.shard_map(
        shards, mesh=mesh, in_specs=in_specs, out_specs=(wide, wide), check_vma=False
    )
```

time: 47.5 us -> 40.8 us (0.86)
  the two profiles are of different devices: /device:TPU:0 before, /device:TPU:9 now
where the time goes in v3:
time: 40.8 us; the launch traced here: 40.5 us
  Pallas kernels  39.9 us (98%)
  between operations  0.64 us (2%)
    pallas_call x1, Pallas kernels, attend(): pl.pallas_call(attention_kernel, grid=(TILES,), in_specs=in_specs, out_sp...  30.7 us
    pallas_call x1, Pallas kernels, pool(): pl.pallas_call(pool_kernel, grid_spec=pltpu.PrefetchScalarGridSpec(num_sc...  9.16 us

profile of v3, /device:TPU:9, one launch (start us, length us, event | category | flops | bytes accessed | tf_op | source)
XLA Modules:
  0.0 40.5 jit_solution(11876394596478627945)
XLA Ops:
  0.6 30.7 %shard_map.167 = (bf16[8192,128]{1,0:T(8,128)(2,1)}, bf16[2048,128]{1,0:T(8,128)(2,1)}, s32[16,128]{1,0:T(8,128)}) custom-call(s32[256]{0:T(256)} %koff.1, bf16[8192,128]{1,0:T(8,128)(2,1)} %atoms_any.1, bf16[8192,128]{1,0:T(8,128)(2,1)} %atoms_any.1, bf16[8192,128]{1,0:T(8,128)(2,1)} %atoms_any.1, bf16[8192,512]{1,0:T(8,128)(2,1)} %bias.1, ...), custom_call_target="tpu_custom_call" | custom-call | flops 6000000000 | bytes 14680064 | tf_op jit(solution)/shard_map/pallas_call | solution.py:285
  31.4 9.2 %shard_map.168 = (bf16[8192,128]{1,0:T(8,128)(2,1)}, f32[1024,384]{1,0:T(8,128)}) custom-call(s32[8192]{0:T(1024)} %tok.1, s32[2048]{0:T(1024)} %bitcast.12, bf16[8192,128]{1,0:T(8,128)(2,1)} %get-tuple-element.6.rows, bf16[2048,128]{1,0:T(8,128)(2,1)} %get-tuple-element.7.far_rows, s32[64,128]{1,0:T(8,128)} %bitcast.6, s32[64,128]{1,0:T(8,128)} %bitcast.9, ...), custom_call_target="tpu_custom_call" | custom-call | flops 5000000000 | bytes 8388608 | tf_op jit(solution)/shard_map/pallas_call | solution.py:398

commit v4 on v3

--- a/solution.py
+++ b/solution.py
@@ -320,111 +320,151 @@
 
 
 def pool_kernel(
-    tok, far_tok, rows, far_rows, ids, mask, far_marks, wp, out, pooled, proj_s, acc_s
+    tokens, ids_any, mask_any, marks_flat, marks_any, rows_any, far_any, wp_any, out, pooled,
+    tok, far_tok, ids, mask, marks, rows, wp, acc_s, pooled_s, sems,
 ):
-    step = pl.program_id(0)
     me = here()
     base = me * TOK_DEV
-
-    @pl.when(step == 0)
-    def _():
-        proj_s[:, C_TOKEN:] = jnp.ones((TILE, 128), jnp.bfloat16)
-        acc_s[...] = jnp.zeros(acc_s.shape, jnp.float32)
-
-    def add_tile(values, token_of, local_of):
-        proj_s[:, :C_TOKEN] = jnp.maximum(dot(values, wp[...]), 0.0).astype(jnp.bfloat16)
-        slots = lax.broadcasted_iota(jnp.int32, (WIN, PART), 0)
-        parts = []
-        for part in range(TILE // PART):
-            local = local_of(part)
-            row = jnp.concatenate([local[i : i + 1] for i in range(PART // 128)], axis=1)
-            start = jnp.clip(((token_of(part * PART) - base) >> 3) << 3, 0, TOK_DEV)
-            end = jnp.minimum(token_of(part * PART + PART - 1) - base, TOK_DEV - 1)
-            parts.append((row, start, (jnp.maximum(end - start, 0) >> 7) + 1))
-
-        def window_sums(part, i):
-            row, start, _ = parts[part]
-            at = pl.multiple_of(start + i * WIN, 8)
-            table = (row - at == slots).astype(jnp.bfloat16)
-            return at, dot(table, proj_s[part * PART : (part + 1) * PART, :])
-
-        for at, sums in [window_sums(part, 0) for part in range(len(parts))]:
-            acc_s[pl.ds(at, WIN), :] += sums
+    copies = [
+        pltpu.make_async_copy(source, target, sems.at[i])
+        for i, (source, target) in enumerate(
+            [
+                (wp_any, wp),
+                (ids_any, ids),
+                (mask_any, mask),
+                (tokens, tok),
+                *[
+                    (rows_any.at[pl.ds(t * TILE, TILE)], rows.at[pl.ds(t * TILE, TILE)])
+                    for t in range(TILES)
+                ],
+                (far_any, rows.at[pl.ds(ATOM_DEV, DRIFT)]),
+                (marks_any, marks),
+                (marks_flat, far_tok),
+                (rows.at[pl.ds(0, ATOM_DEV)], out),
+                *[
+                    (pooled_s.at[pl.ds(i * WIN, WIN)], pooled.at[pl.ds(i * WIN, WIN)])
+                    for i in range(TOK_DEV // WIN)
+                ],
+            ]
+        )
+    ]
+    early, tiles, late = copies[:4], copies[4 : 4 + TILES], copies[4 + TILES : 7 + TILES]
+    through, results = copies[7 + TILES], copies[8 + TILES :]
+    for copy in [tiles[0], *early, *tiles[1:], *late]:
+        copy.start()
+    acc_s[...] = jnp.zeros(acc_s.shape, jnp.float32)
+    for copy in early:
+        copy.wait()
+    slots = lax.broadcasted_iota(jnp.int32, (WIN, PART), 0)
+    ones = jnp.ones((PART, 128), jnp.bfloat16)
+    per = PART // 128
+
+    def project(values):
+        return jnp.maximum(dot(values, wp[...]), 0.0).astype(jnp.bfloat16)
+
+    def window_sums(row, at, projected):
+        table = (row - at == slots).astype(jnp.bfloat16)
+        return dot(table, jnp.concatenate([projected, ones], axis=1))
+
+    def part_of(local, head, tail):
+        row = jnp.concatenate([local[i : i + 1] for i in range(per)], axis=1)
+        start = jnp.clip(((head - base) >> 3) << 3, 0, TOK_DEV)
+        end = jnp.minimum(tail - base, TOK_DEV - 1)
+        return row, start, (jnp.maximum(end - start, 0) >> 7) + 1
+
+    def own_part(part):
+        at = slice(part * per, (part + 1) * per)
+        local = jnp.where(mask[at, :] == 1, ids[at, :] - base, -1)
+        return part_of(local, tok[part * PART], tok[part * PART + PART - 1])
+
+    def far_part(part):
+        mark = marks[part * per : (part + 1) * per, :]
+        local = jnp.where(mark & 1 == 1, (mark >> 1) - base, -1)
+        return part_of(local, far_tok[part * PART] >> 1, far_tok[part * PART + PART - 1] >> 1)
+
+    def first_windows(parts, first_row):
+        count = len(parts)
+        projected = project(rows[first_row : first_row + count * PART, :])
+        for i, (row, start, _) in enumerate(parts):
+            at = pl.multiple_of(start, 8)
+            acc_s[pl.ds(at, WIN), :] += window_sums(
+                row, at, projected[i * PART : (i + 1) * PART]
+            )
+
+    def other_windows(parts, first_row):
         most = parts[0][2]
-        for _, _, n in parts[1:]:
-            most = jnp.maximum(most, n)
+        for _, _, windows in parts[1:]:
+            most = jnp.maximum(most, windows)
 
         @pl.when(most > 1)
         def _():
-            for part in range(len(parts)):
-
-                def add(i, carry, part=part):
-                    at, sums = window_sums(part, i)
-                    acc_s[pl.ds(at, WIN), :] += sums
-                    return carry
-
-                lax.fori_loop(1, parts[part][2], add, 0)
-
-    per = PART // 128
-
-    @pl.when(step < TILES)
-    def _():
-        def local_of(part):
-            at = pl.ds(step * (TILE // 128) + part * per, per)
-            return jnp.where(mask[at, :] == 1, ids[at, :] - base, -1)
-
-        out[...] = rows[...]
-        add_tile(rows[...], lambda a: tok[step * TILE + a], local_of)
-
-    @pl.when((step == TILES) & (me > 0))
-    def _():
-        def local_of(part):
-            mark = far_marks[part * per : (part + 1) * per, :]
-            return jnp.where(mark & 1 == 1, (mark >> 1) - base, -1)
-
-        add_tile(far_rows[...], lambda a: far_tok[a] >> 1, local_of)
-
-    @pl.when(step == TILES)
-    def _():
-        counts = jnp.maximum(acc_s[0:TOK_DEV, C_TOKEN:], 1.0)
-        pooled[...] = acc_s[0:TOK_DEV, :C_TOKEN] / jnp.concatenate(
+            for i, (row, start, windows) in enumerate(parts):
+                at_row = first_row + i * PART
+
+                @pl.when(windows > 1)
+                def _(row=row, start=start, windows=windows, at_row=at_row):
+                    projected = project(rows[at_row : at_row + PART, :])
+
+                    def add(i, carry):
+                        at = pl.multiple_of(start + i * WIN, 8)
+                        acc_s[pl.ds(at, WIN), :] += window_sums(row, at, projected)
+                        return carry
+
+                    lax.fori_loop(1, windows, add, 0)
+
+    own = [own_part(part) for part in range(ATOM_DEV // PART)]
+    for t in range(TILES):
+        tiles[t].wait()
+        first_windows(own[t * TILE // PART : (t + 1) * TILE // PART], t * TILE)
+    through.start()
+    other_windows(own, 0)
+    for copy in late:
+        copy.wait()
+
+    @pl.when(me > 0)
+    def _():
+        far = [far_part(part) for part in range(DRIFT // PART)]
+        first_windows(far, ATOM_DEV)
+        other_windows(far, ATOM_DEV)
+
+    for i, copy in enumerate(results):
+        at = slice(i * WIN, (i + 1) * WIN)
+        counts = jnp.maximum(acc_s[at, C_TOKEN:], 1.0)
+        pooled_s[at, :] = acc_s[at, :C_TOKEN] / jnp.concatenate(
             [counts] * (C_TOKEN // 128), axis=1
         )
+        copy.start()
+    for copy in [*results, through]:
+        copy.wait()
 
 
 def pool(tokens, ids2, mask2, far_marks, rows, far_rows, w_pool):
-    whole = lambda shape: pl.BlockSpec(shape, lambda t, *_: (0,) * len(shape))
-    tiles = pl.BlockSpec((TILE, C_ATOM), lambda t, *_: (jnp.minimum(t, TILES - 1), 0))
+    anywhere = pl.BlockSpec(memory_space=pl.ANY)
     return pl.pallas_call(
         pool_kernel,
-        grid_spec=pltpu.PrefetchScalarGridSpec(
-            num_scalar_prefetch=2,
-            grid=(TILES + 1,),
-            in_specs=[
-                tiles,
-                whole(far_rows.shape),
-                whole(ids2.shape),
-                whole(mask2.shape),
-                whole(far_marks.shape),
-                whole(w_pool.shape),
-            ],
-            out_specs=[tiles, whole((TOK_DEV, C_TOKEN))],
-            scratch_shapes=[
-                pltpu.VMEM((TILE, SUM_COLS), jnp.bfloat16),
-                pltpu.VMEM((ACC_ROWS, SUM_COLS), jnp.float32),
-            ],
-        ),
+        in_specs=[anywhere] * 8,
+        out_specs=[anywhere] * 2,
         out_shape=[
             jax.ShapeDtypeStruct((ATOM_DEV, C_ATOM), jnp.bfloat16),
             jax.ShapeDtypeStruct((TOK_DEV, C_TOKEN), jnp.float32),
         ],
-        compiler_params=pltpu.CompilerParams(
-            dimension_semantics=("arbitrary",), vmem_limit_bytes=VMEM_BYTES
-        ),
+        scratch_shapes=[
+            pltpu.SMEM((ATOM_DEV,), jnp.int32),
+            pltpu.SMEM((DRIFT,), jnp.int32),
+            pltpu.VMEM((MASK_ROWS, 128), jnp.int32),
+            pltpu.VMEM((MASK_ROWS, 128), jnp.int32),
+            pltpu.VMEM((FAR, 128), jnp.int32),
+            pltpu.VMEM((ATOM_DEV + DRIFT, C_ATOM), jnp.bfloat16),
+            pltpu.VMEM((C_ATOM, C_TOKEN), jnp.bfloat16),
+            pltpu.VMEM((ACC_ROWS, SUM_COLS), jnp.float32),
+            pltpu.VMEM((TOK_DEV, C_TOKEN), jnp.float32),
+            pltpu.SemaphoreType.DMA((8 + TILES + TOK_DEV // WIN,)),
+        ],
+        compiler_params=pltpu.CompilerParams(vmem_limit_bytes=VMEM_BYTES),
         cost_estimate=pl.CostEstimate(
             flops=5 * 10**9, bytes_accessed=8 * 2**20, transcendentals=0
         ),
-    )(tokens, far_marks.reshape(-1), rows, far_rows, ids2, mask2, far_marks, w_pool)
+    )(tokens, ids2, mask2, far_marks.reshape(-1), far_marks, rows, far_rows, w_pool)
 
 
 def shards(

time: 40.8 us -> 38.4 us (0.941)
  Pallas kernels: 39.9 us -> 37.7 us
    pallas_call x1, Pallas kernels: 9.16 us -> 6.98 us  [pool(): pl.pallas_call(pool_kernel, in_specs=[anywhere] * 8, out_specs=[anywhere]...]
where the time goes in v4:
time: 38.4 us; the launch traced here: 38.3 us
  Pallas kernels  37.7 us (98%)
  between operations  0.64 us (2%)
    pallas_call x1, Pallas kernels, attend(): pl.pallas_call(attention_kernel, grid=(TILES,), in_specs=in_specs, out_sp...  30.7 us
    pallas_call x1, Pallas kernels, pool(): pl.pallas_call(pool_kernel, in_specs=[anywhere] * 8, out_specs=[anywhere]...  6.98 us

profile of v4, /device:TPU:9, one launch (start us, length us, event | category | flops | bytes accessed | tf_op | source)
XLA Modules:
  0.0 38.3 jit_solution(1795793322528187196)
XLA Ops:
  0.6 30.7 %shard_map.167 = (bf16[8192,128]{1,0:T(8,128)(2,1)}, bf16[2048,128]{1,0:T(8,128)(2,1)}, s32[16,128]{1,0:T(8,128)}) custom-call(s32[256]{0:T(256)} %koff.1, bf16[8192,128]{1,0:T(8,128)(2,1)} %atoms_any.1, bf16[8192,128]{1,0:T(8,128)(2,1)} %atoms_any.1, bf16[8192,128]{1,0:T(8,128)(2,1)} %atoms_any.1, bf16[8192,512]{1,0:T(8,128)(2,1)} %bias.1, ...), custom_call_target="tpu_custom_call" | custom-call | flops 6000000000 | bytes 14680064 | tf_op jit(solution)/shard_map/pallas_call | solution.py:285
  31.4 7.0 %shard_map.168 = (bf16[8192,128]{1,0:T(8,128)(2,1)}, f32[1024,384]{1,0:T(8,128)}) custom-call(s32[8192]{0:T(1024)} %tokens.1, s32[64,128]{1,0:T(8,128)} %bitcast.6, s32[64,128]{1,0:T(8,128)} %bitcast.9, s32[2048]{0:T(1024)} %bitcast.12, s32[16,128]{1,0:T(8,128)} %get-tuple-element.5.marks_any, bf16[8192,128]{1,0:T(8,128)(2,1)} %get-tuple-element.6.rows_any, ...), custom_call_target="tpu_custom_call" | custom-call | flops 5000000000 | bytes 8388608 | tf_op jit(solution)/shard_map/pallas_call | solution.py:443

commit v5 on v4

--- a/solution.py
+++ b/solution.py
@@ -33,6 +33,7 @@
 PEN_OFF = 8
 MASK_ROWS = ATOM_DEV // 128
 FAR = DRIFT // 128
+END = 128
 PEN_ROWS = MASK_ROWS + 2 * PEN_OFF
 QSCALE = 1.0 / math.sqrt(HEAD)
 
@@ -63,7 +64,7 @@
 
 
 def tile_of(step):
-    return jnp.where(step == 0, 1, jnp.where(step == 1, 3, jnp.where(step == 2, 2, 0)))
+    return jnp.where(step == 0, 3, jnp.where(step == 3, 0, step))
 
 
 def here():
@@ -76,11 +77,11 @@
 
 
 def attention_kernel(
-    koff, cur, prev, nxt, bias, mask, ids,
+    koff, cur, prev, nxt, bias, mask, ids, end_rows, near_end, end_bias,
     g1, wq, wk, wv, wg, wo, g2, wfg, wfu, wfd,
     atoms_any, mask_any,
-    out, got_rows, got_marks,
-    k_s, v_s, pen_s, q_s, gate_s, att_s, send_s, low, high, below, above,
+    out, end_out, got_rows, got_marks,
+    k_s, v_s, pen_s, q_s, gate_s, att_s, send_s, send_end, low, high, below, above,
     below_mask, above_mask, marks_s, send_sem, recv_sem,
 ):
     step = pl.program_id(0)
@@ -108,7 +109,12 @@
         remote(atoms_any.at[pl.ds(0, REACH)], above, 1, left),
         remote(mask_any.at[pl.ds(0, 8)], above_mask, 3, left),
     ]
-    tails = [remote(marks_s, got_marks, 4, right), remote(send_s, got_rows, 5, right)]
+    main = pl.ds(0, DRIFT - END)
+    tails = [
+        remote(marks_s, got_marks, 4, right),
+        remote(send_s.at[main], got_rows.at[main], 5, right),
+        remote(send_end, got_rows.at[pl.ds(DRIFT - END, END)], 6, right),
+    ]
     has_right, has_left = me < devices - 1, me > 0
 
     @pl.when(step == 0)
@@ -130,52 +136,6 @@
         low[...] = jnp.zeros((REACH, C_ATOM), jnp.bfloat16)
         high[...] = jnp.zeros((REACH, C_ATOM), jnp.bfloat16)
         marks_s[...] = ids[...] * 2 + mask[MASK_ROWS - FAR :, :]
-
-    @pl.when(step == 1)
-    def _():
-        @pl.when(has_left)
-        def _():
-            for copy in ups:
-                copy.wait_recv()
-            low[...] = below[...]
-            pen_s[0:PEN_OFF, :] = jnp.where(below_mask[...] == 1, LIVE, MASKED)
-            for copy in downs:
-                copy.wait_send()
-
-        @pl.when(has_right)
-        def _():
-            for copy in downs:
-                copy.wait_recv()
-            high[...] = above[...]
-            pen_s[PEN_ROWS - PEN_OFF :, :] = jnp.where(above_mask[...] == 1, LIVE, MASKED)
-            for copy in ups:
-                copy.wait_send()
-
-    first = jnp.where(tile == 0, low[...], prev[...])
-    last = jnp.where(tile == TILES - 1, high[...], nxt[...])
-    normed = layer_norm(jnp.concatenate([first, cur[...], last], axis=0), g1[...])
-    kv = dot(normed, jnp.concatenate([wk[...], wv[...]], axis=1))
-    k_s[...] = kv[:, :C_ATOM]
-    v_s[...] = kv[:, C_ATOM:]
-    qg = dot(normed[REACH : REACH + TILE], jnp.concatenate([wq[...], wg[...]], axis=1))
-    q_s[...] = (qg[:, :C_ATOM] * QSCALE).astype(jnp.bfloat16)
-    gate_s[...] = sigmoid(qg[:, C_ATOM:])
-
-    @pl.when(step == 0)
-    def _():
-        barrier = pltpu.get_barrier_semaphore()
-        pl.semaphore_wait(barrier, has_right.astype(jnp.int32) + has_left.astype(jnp.int32))
-
-        @pl.when(has_right)
-        def _():
-            for copy in ups:
-                copy.start()
-            tails[0].start()
-
-        @pl.when(has_left)
-        def _():
-            for copy in downs:
-                copy.start()
 
     lane = lax.broadcasted_iota(jnp.int32, (1, C_ATOM), 1)
     heads = [(lane // HEAD == h) for h in range(HEADS)]
@@ -186,72 +146,131 @@
     ).astype(jnp.bfloat16)
     ones = jnp.ones((KEY_WINDOW, 128), jnp.bfloat16)
 
-    offs = [
-        jnp.clip(koff[tile * BLOCKS + blk], -REACH, -QUERY_BLOCK) for blk in range(BLOCKS)
-    ]
-    rows = [slice(blk * QUERY_BLOCK, (blk + 1) * QUERY_BLOCK) for blk in range(BLOCKS)]
-    windows = [
-        pl.ds(blk * QUERY_BLOCK + REACH + offs[blk], KEY_WINDOW) for blk in range(BLOCKS)
-    ]
-    scores, limits, weights, mixes = {}, {}, {}, {}
-
-    def score(blk):
-        keys = k_s[windows[blk], :].astype(jnp.bfloat16)
-        q = q_s[rows[blk], :]
-        stacked = jnp.concatenate([q * m for m in head_ones], axis=0)
-        biases = jnp.concatenate(
-            [
-                bias[rows[blk], h * KEY_WINDOW : (h + 1) * KEY_WINDOW]
-                for h in range(HEADS)
-            ],
-            axis=0,
-        )
-        scores[blk] = lax.dot_general(
-            jnp.concatenate([stacked, biases], axis=1),
-            jnp.concatenate([keys, eye], axis=1),
-            NT,
-            preferred_element_type=jnp.float32,
-        )
-        place = tile * TILE + (blk * QUERY_BLOCK + PEN_OFF * 128) + offs[blk]
-        turn = 128 - (place & 127)
-        pair = pen_s[pl.ds(place >> 7, 2), :]
-        turned = pltpu.roll(pair, turn & 127, 1)
-        limits[blk] = jnp.where(lane < turn, turned[0:1], turned[1:2])
-
-    def soften(blk):
-        held = jnp.minimum(scores.pop(blk), limits.pop(blk))
-        top = jnp.max(held, axis=1, keepdims=True)
-        weights[blk] = jnp.exp(held - top).astype(jnp.bfloat16)
-
-    def mix(blk):
-        values = v_s[windows[blk], :].astype(jnp.bfloat16)
-        mixes[blk] = dot(weights.pop(blk), jnp.concatenate([values, ones], axis=1))
-
-    def finish(blk):
-        mixed = mixes.pop(blk)
-        num = mixed[0:QUERY_BLOCK, :C_ATOM]
-        den = mixed[0:QUERY_BLOCK, C_ATOM:]
-        for h in range(1, HEADS):
-            part = mixed[h * QUERY_BLOCK : (h + 1) * QUERY_BLOCK]
-            num = jnp.where(heads[h], part[:, :C_ATOM], num)
-            den = jnp.where(heads[h], part[:, C_ATOM:], den)
-        att_s[rows[blk], :] = (num / den * gate_s[rows[blk], :]).astype(jnp.bfloat16)
-
-    for stage in (score, soften, mix, finish):
-        for blk in range(BLOCKS):
-            stage(blk)
-
-    updated = (cur[...].astype(jnp.float32) + dot(att_s[...], wo[...])).astype(jnp.bfloat16)
-    second = layer_norm(updated, g2[...])
-    gated = dot(second, wfg[...])
-    hidden = (gated * sigmoid(gated) * dot(second, wfu[...])).astype(jnp.bfloat16)
-    atom_out = (updated.astype(jnp.float32) + dot(hidden, wfd[...])).astype(jnp.bfloat16)
-    out[...] = atom_out
-
-    @pl.when((step == 1) & has_right)
-    def _():
-        send_s[...] = out[...]
-        tails[1].start()
+    def block_out(rows_in, bias_ref, row0, count):
+        blocks = count // QUERY_BLOCK
+        middle = rows_in[REACH : REACH + count]
+        normed = layer_norm(rows_in, g1[...])
+        kv = dot(normed, jnp.concatenate([wk[...], wv[...]], axis=1))
+        k_s[0 : count + 2 * REACH, :] = kv[:, :C_ATOM]
+        v_s[0 : count + 2 * REACH, :] = kv[:, C_ATOM:]
+        qg = dot(normed[REACH : REACH + count], jnp.concatenate([wq[...], wg[...]], axis=1))
+        q_s[0:count, :] = (qg[:, :C_ATOM] * QSCALE).astype(jnp.bfloat16)
+        gate_s[0:count, :] = sigmoid(qg[:, C_ATOM:])
+
+        offs = [
+            jnp.clip(koff[row0 // QUERY_BLOCK + blk], -REACH, -QUERY_BLOCK) for blk in range(blocks)
+        ]
+        rows = [slice(blk * QUERY_BLOCK, (blk + 1) * QUERY_BLOCK) for blk in range(blocks)]
+        windows = [
+            pl.ds(blk * QUERY_BLOCK + REACH + offs[blk], KEY_WINDOW) for blk in range(blocks)
+        ]
+        scores, limits, weights, mixes = {}, {}, {}, {}
+
+        def score(blk):
+            keys = k_s[windows[blk], :].astype(jnp.bfloat16)
+            q = q_s[rows[blk], :]
+            stacked = jnp.concatenate([q * m for m in head_ones], axis=0)
+            biases = jnp.concatenate(
+                [
+                    bias_ref[rows[blk], h * KEY_WINDOW : (h + 1) * KEY_WINDOW]
+                    for h in range(HEADS)
+                ],
+                axis=0,
+            )
+            scores[blk] = lax.dot_general(
+                jnp.concatenate([stacked, biases], axis=1),
+                jnp.concatenate([keys, eye], axis=1),
+                NT,
+                preferred_element_type=jnp.float32,
+            )
+            place = row0 + (blk * QUERY_BLOCK + PEN_OFF * 128) + offs[blk]
+            turn = 128 - (place & 127)
+            pair = pen_s[pl.ds(place >> 7, 2), :]
+            turned = pltpu.roll(pair, turn & 127, 1)
+            limits[blk] = jnp.where(lane < turn, turned[0:1], turned[1:2])
+
+        def soften(blk):
+            held = jnp.minimum(scores.pop(blk), limits.pop(blk))
+            top = jnp.max(held, axis=1, keepdims=True)
+            weights[blk] = jnp.exp(held - top).astype(jnp.bfloat16)
+
+        def mix(blk):
+            values = v_s[windows[blk], :].astype(jnp.bfloat16)
+            mixes[blk] = dot(weights.pop(blk), jnp.concatenate([values, ones], axis=1))
+
+        def finish(blk):
+            mixed = mixes.pop(blk)
+            num = mixed[0:QUERY_BLOCK, :C_ATOM]
+            den = mixed[0:QUERY_BLOCK, C_ATOM:]
+            for h in range(1, HEADS):
+                part = mixed[h * QUERY_BLOCK : (h + 1) * QUERY_BLOCK]
+                num = jnp.where(heads[h], part[:, :C_ATOM], num)
+                den = jnp.where(heads[h], part[:, C_ATOM:], den)
+            att_s[rows[blk], :] = (num / den * gate_s[rows[blk], :]).astype(jnp.bfloat16)
+
+        for stage in (score, soften, mix, finish):
+            for blk in range(blocks):
+                stage(blk)
+
+        mixed = dot(att_s[0:count, :], wo[...])
+        updated = (middle.astype(jnp.float32) + mixed).astype(jnp.bfloat16)
+        second = layer_norm(updated, g2[...])
+        gated = dot(second, wfg[...])
+        hidden = (gated * sigmoid(gated) * dot(second, wfu[...])).astype(jnp.bfloat16)
+        return (updated.astype(jnp.float32) + dot(hidden, wfd[...])).astype(jnp.bfloat16)
+
+    first = jnp.where(tile == 0, low[...], prev[...])
+    last = jnp.where(tile == TILES - 1, high[...], nxt[...])
+    rows_in = jnp.concatenate([first, cur[...], last], axis=0)
+    out[...] = block_out(rows_in, bias, tile * TILE, TILE)
+
+    @pl.when(step == 0)
+    def _():
+        barrier = pltpu.get_barrier_semaphore()
+        pl.semaphore_wait(barrier, has_right.astype(jnp.int32) + has_left.astype(jnp.int32))
+
+        @pl.when(has_right)
+        def _():
+            for copy in ups:
+                copy.start()
+            send_s[...] = out[...]
+            for copy in tails[:2]:
+                copy.start()
+
+        @pl.when(has_left)
+        def _():
+            for copy in downs:
+                copy.start()
+
+    @pl.when(step == 1)
+    def _():
+        @pl.when(has_left)
+        def _():
+            for copy in ups:
+                copy.wait_recv()
+            low[...] = below[...]
+            pen_s[0:PEN_OFF, :] = jnp.where(below_mask[...] == 1, LIVE, MASKED)
+            for copy in downs:
+                copy.wait_send()
+
+        @pl.when(has_right)
+        def _():
+            for copy in downs:
+                copy.wait_recv()
+            high[...] = above[...]
+            pen_s[PEN_ROWS - PEN_OFF :, :] = jnp.where(above_mask[...] == 1, LIVE, MASKED)
+            for copy in ups:
+                copy.wait_send()
+
+    @pl.when(step == 1)
+    def _():
+        rows_in = jnp.concatenate([near_end[...], end_rows[...], high[...]], axis=0)
+        send_end[...] = block_out(rows_in, end_bias, ATOM_DEV - END, END)
+        end_out[...] = send_end[...]
+
+        @pl.when(has_right)
+        def _():
+            tails[2].start()
 
     @pl.when((step == TILES - 1) & has_right)
     def _():
@@ -278,6 +297,9 @@
         tiles(HEADS * KEY_WINDOW),
         whole(mask2.shape),
         pl.BlockSpec((FAR, 128), lambda t: (MASK_ROWS // FAR - 1, 0)),
+        pl.BlockSpec((END, C_ATOM), lambda t: (ATOM_DEV // END - 1, 0)),
+        pl.BlockSpec((REACH, C_ATOM), lambda t: ((ATOM_DEV - END) // REACH - 1, 0)),
+        pl.BlockSpec((END, HEADS * KEY_WINDOW), lambda t: (ATOM_DEV // END - 1, 0)),
         *[whole(w.shape) for w in weights],
         anywhere,
         anywhere,
@@ -286,9 +308,10 @@
         attention_kernel,
         grid=(TILES,),
         in_specs=in_specs,
-        out_specs=[tiles(C_ATOM), anywhere, anywhere],
+        out_specs=[tiles(C_ATOM), whole((END, C_ATOM)), anywhere, anywhere],
         out_shape=[
             jax.ShapeDtypeStruct((ATOM_DEV, C_ATOM), jnp.bfloat16),
+            jax.ShapeDtypeStruct((END, C_ATOM), jnp.bfloat16),
             jax.ShapeDtypeStruct((DRIFT, C_ATOM), jnp.bfloat16),
             jax.ShapeDtypeStruct((FAR, 128), jnp.int32),
         ],
@@ -300,12 +323,13 @@
             pltpu.VMEM((TILE, C_ATOM), jnp.float32),
             pltpu.VMEM((TILE, C_ATOM), jnp.bfloat16),
             pltpu.VMEM((DRIFT, C_ATOM), jnp.bfloat16),
+            pltpu.VMEM((END, C_ATOM), jnp.bfloat16),
             *[pltpu.VMEM((REACH, C_ATOM), jnp.bfloat16) for _ in range(4)],
             pltpu.VMEM((8, 128), jnp.int32),
             pltpu.VMEM((8, 128), jnp.int32),
             pltpu.VMEM((FAR, 128), jnp.int32),
-            pltpu.SemaphoreType.DMA((6,)),
-            pltpu.SemaphoreType.DMA((6,)),
+            pltpu.SemaphoreType.DMA((7,)),
+            pltpu.SemaphoreType.DMA((7,)),
         ],
         compiler_params=pltpu.CompilerParams(
             dimension_semantics=("arbitrary",),
@@ -316,11 +340,11 @@
         cost_estimate=pl.CostEstimate(
             flops=6 * 10**9, bytes_accessed=14 * 2**20, transcendentals=6 * 10**6
         ),
-    )(key_offsets, atoms, atoms, atoms, pair_bias, mask2, ids2, *weights, atoms, mask2)
+    )(key_offsets, atoms, atoms, atoms, pair_bias, mask2, ids2, atoms, atoms, pair_bias, *weights, atoms, mask2)
 
 
 def pool_kernel(
-    tokens, ids_any, mask_any, marks_flat, marks_any, rows_any, far_any, wp_any, out, pooled,
+    tokens, ids_any, mask_any, marks_flat, marks_any, rows_any, end_any, far_any, wp_any, out, pooled,
     tok, far_tok, ids, mask, marks, rows, wp, acc_s, pooled_s, sems,
 ):
     me = here()
@@ -334,9 +358,10 @@
                 (mask_any, mask),
                 (tokens, tok),
                 *[
-                    (rows_any.at[pl.ds(t * TILE, TILE)], rows.at[pl.ds(t * TILE, TILE)])
-                    for t in range(TILES)
+                    (rows_any.at[pl.ds(t * TILE, size)], rows.at[pl.ds(t * TILE, size)])
+                    for t, size in enumerate([TILE] * (TILES - 1) + [TILE - END])
                 ],
+                (end_any, rows.at[pl.ds(ATOM_DEV - END, END)]),
                 (far_any, rows.at[pl.ds(ATOM_DEV, DRIFT)]),
                 (marks_any, marks),
                 (marks_flat, far_tok),
@@ -348,9 +373,9 @@
             ]
         )
     ]
-    early, tiles, late = copies[:4], copies[4 : 4 + TILES], copies[4 + TILES : 7 + TILES]
-    through, results = copies[7 + TILES], copies[8 + TILES :]
-    for copy in [tiles[0], *early, *tiles[1:], *late]:
+    early, tiles, end = copies[:4], copies[4 : 4 + TILES], copies[4 + TILES]
+    late, through, results = copies[5 + TILES : 8 + TILES], copies[8 + TILES], copies[9 + TILES :]
+    for copy in [tiles[0], *early, *tiles[1:], end, *late]:
         copy.start()
     acc_s[...] = jnp.zeros(acc_s.shape, jnp.float32)
     for copy in early:
@@ -415,6 +440,8 @@
     own = [own_part(part) for part in range(ATOM_DEV // PART)]
     for t in range(TILES):
         tiles[t].wait()
+        if t == TILES - 1:
+            end.wait()
         first_windows(own[t * TILE // PART : (t + 1) * TILE // PART], t * TILE)
     through.start()
     other_windows(own, 0)
@@ -438,11 +465,11 @@
         copy.wait()
 
 
-def pool(tokens, ids2, mask2, far_marks, rows, far_rows, w_pool):
+def pool(tokens, ids2, mask2, far_marks, rows, end_rows, far_rows, w_pool):
     anywhere = pl.BlockSpec(memory_space=pl.ANY)
     return pl.pallas_call(
         pool_kernel,
-        in_specs=[anywhere] * 8,
+        in_specs=[anywhere] * 9,
         out_specs=[anywhere] * 2,
         out_shape=[
             jax.ShapeDtypeStruct((ATOM_DEV, C_ATOM), jnp.bfloat16),
@@ -458,13 +485,13 @@
             pltpu.VMEM((C_ATOM, C_TOKEN), jnp.bfloat16),
             pltpu.VMEM((ACC_ROWS, SUM_COLS), jnp.float32),
             pltpu.VMEM((TOK_DEV, C_TOKEN), jnp.float32),
-            pltpu.SemaphoreType.DMA((8 + TILES + TOK_DEV // WIN,)),
+            pltpu.SemaphoreType.DMA((9 + TILES + TOK_DEV // WIN,)),
         ],
         compiler_params=pltpu.CompilerParams(vmem_limit_bytes=VMEM_BYTES),
         cost_estimate=pl.CostEstimate(
             flops=5 * 10**9, bytes_accessed=8 * 2**20, transcendentals=0
         ),
-    )(tokens, ids2, mask2, far_marks.reshape(-1), far_marks, rows, far_rows, w_pool)
+    )(tokens, ids2, mask2, far_marks.reshape(-1), far_marks, rows, end_rows, far_rows, w_pool)
 
 
 def shards(
@@ -499,8 +526,8 @@
         w_ff_up,
         w_ff_down,
     )
-    rows, far_rows, far_marks = attend(key_offsets, atoms, pair_bias, mask2, ids2, weights)
-    return tuple(pool(atom_token, ids2, mask2, far_marks, rows, far_rows, w_pool))
+    rows, end_rows, far_rows, far_marks = attend(key_offsets, atoms, pair_bias, mask2, ids2, weights)
+    return tuple(pool(atom_token, ids2, mask2, far_marks, rows, end_rows, far_rows, w_pool))
 
 
 def solution(mesh):

time: 38.4 us -> 39.5 us (1.029)
  the two profiles are of different devices: /device:TPU:9 before, /device:TPU:23 now
where the time goes in v5:
time: 39.5 us; the launch traced here: 39.3 us
  Pallas kernels  38.7 us (98%)
  between operations  0.64 us (2%)
    pallas_call x1, Pallas kernels, attend(): pl.pallas_call(attention_kernel, grid=(TILES,), in_specs=in_specs, out_sp...  31.7 us
    pallas_call x1, Pallas kernels, pool(): pl.pallas_call(pool_kernel, in_specs=[anywhere] * 9, out_specs=[anywhere]...  6.99 us

profile of v5, /device:TPU:23, one launch (start us, length us, event | category | flops | bytes accessed | tf_op | source)
XLA Modules:
  0.0 39.3 jit_solution(14711218192560657483)
XLA Ops:
  0.6 31.7 %shard_map.167 = (bf16[8192,128]{1,0:T(8,128)(2,1)}, bf16[128,128]{1,0:T(8,128)(2,1)}, bf16[2048,128]{1,0:T(8,128)(2,1)}, s32[16,128]{1,0:T(8,128)}) custom-call(s32[256]{0:T(256)} %koff.1, bf16[8192,128]{1,0:T(8,128)(2,1)} %atoms_any.1, bf16[8192,128]{1,0:T(8,128)(2,1)} %atoms_any.1, bf16[8192,128]{1,0:T(8,128)(2,1)} %atoms_any.1, ...), custom_call_target="tpu_custom_call" | custom-call | flops 6000000000 | bytes 14680064 | tf_op jit(solution)/shard_map/pallas_call | solution.py:307
  32.3 7.0 %shard_map.168 = (bf16[8192,128]{1,0:T(8,128)(2,1)}, f32[1024,384]{1,0:T(8,128)}) custom-call(s32[8192]{0:T(1024)} %tokens.1, s32[64,128]{1,0:T(8,128)} %bitcast.9, s32[64,128]{1,0:T(8,128)} %bitcast.7, s32[2048]{0:T(1024)} %bitcast.12, s32[16,128]{1,0:T(8,128)} %get-tuple-element.6.marks_any, bf16[8192,128]{1,0:T(8,128)(2,1)} %get-tuple-element.7.rows_any, ...), custom_call_target="tpu_custom_call" | custom-call | flops 5000000000 | bytes 8388608 | tf_op jit(solution)/shard_map/pallas_call | solution.py:470
